TPU v7x, 128 devices: a whole 4x4x4 slice. The times are simulated.
128 devices in a mesh: seq: 32 (over z, y, core), rep: 4 (over x).
Axes of the slice: x: 4, y: 4, z: 4, core: 2. Of those that a mesh axis runs over, the one named last changes fastest.
Arguments:
- queries: bfloat16 [4, 8192, 512], P('rep', 'seq'), may hold values from -6 to 6
- key_vectors: bfloat16 [4, 8192, 128], P('rep', 'seq'), may hold values from -6 to 6
- values: bfloat16 [4, 8192, 128], P('rep', 'seq'), may hold values from -6 to 6
- forget_logit: bfloat16 [4, 4, 8192], P('rep', None, 'seq'), may hold values from 0 to 11
- out_grad: bfloat16 [4, 8192, 512], P('rep', 'seq'), may hold values from -6 to 6
- query_gain: float32 [128], replicated, may hold values from 0.1 to 1.9
- key_gain: float32 [128], replicated, may hold values from 0.1 to 1.9
- lengths: int32 [4, 4], P('rep'), may hold values from 1 to 96, 128 in all within a row
Outputs:
- attention: bfloat16 [4, 8192, 512], P('rep', 'seq')
- query_grad: bfloat16 [4, 8192, 512], P('rep', 'seq')
- key_grad: bfloat16 [4, 8192, 128], P('rep', 'seq')
- value_grad: bfloat16 [4, 8192, 128], P('rep', 'seq')
- forget_grad: float32 [4, 4, 8192], P('rep', None, 'seq')
- norm_gain_grad: float32 [2, 128], replicated
Inputs may be any that keep to these rules, and one draw needn't show every extreme that they name: `lengths`: each row lists the documents of one pack in order, in tiles of 64 tokens, and sums to 128.
All inputs are finite; a program needn't handle non-finite values.
Results may differ from a plain program's by a relative error of at most 0.02.
Values may be sent and summed in bfloat16 or wider, within the bound.
A program may use at most 64 MiB of HBM per device.

v0:
```python
import jax
import jax.numpy as jnp
from jax import lax
from jax.sharding import PartitionSpec as P

TILE = 64


norm_eps = 1e-06
key_span = 512


def norm_rows(raw_values, gain_vec, factor):
    lifted = raw_values.astype(jnp.float32)
    mean_square = jnp.mean(lifted * lifted, axis=-1, keepdims=True)
    return lifted * lax.rsqrt(mean_square + norm_eps) * (gain_vec * factor)


def tile_starts(lengths_row, tile_count):
    doc_ends = jnp.cumsum(lengths_row)
    tile_index = jnp.arange(tile_count, dtype=jnp.int32)
    passed = doc_ends[None, :] <= tile_index[:, None]
    return jnp.sum(jnp.where(passed, lengths_row[None, :], 0), axis=1)


def pad_rows(array_in, along):
    widths = [(0, 0)] * array_in.ndim
    widths[along] = (0, key_span)
    return jnp.pad(array_in, widths)


def prepare(gathered):
    key_all, value_all, logit_all = gathered
    gate = jnp.cumsum(jax.nn.log_sigmoid(logit_all.astype(jnp.float32)), axis=1)
    return (pad_rows(key_all, 0), pad_rows(value_all, 0), pad_rows(gate, 1))


def contract_last(left_rows, right_rows):
    return lax.dot_general(
        left_rows, right_rows, (((1,), (1,)), ((), ())), preferred_element_type=jnp.float32
    )


def contract_first(left_rows, right_rows):
    return lax.dot_general(
        left_rows, right_rows, (((0,), (0,)), ((), ())), preferred_element_type=jnp.float32
    )


def block_scores(
    query_rows, key_pad, gate_pad, query_gate, block_first, tile_first, doc_first, head_count
):
    key_block = lax.dynamic_slice_in_dim(key_pad, block_first, key_span, 0)
    scores = contract_last(query_rows, key_block)
    row_count = query_rows.shape[0] // head_count
    scores = scores.reshape(head_count, row_count, key_span)
    key_gate = lax.dynamic_slice_in_dim(gate_pad, block_first, key_span, 1)
    scores = scores + query_gate[:, :, None] - key_gate[:, None, :]
    key_place = block_first + jnp.arange(key_span, dtype=jnp.int32)
    query_place = tile_first + jnp.arange(row_count, dtype=jnp.int32)
    allowed = (key_place[None, :] >= doc_first) & (key_place[None, :] <= query_place[:, None])
    return (jnp.where(allowed[None, :, :], scores, -jnp.inf), key_block)


def query_setup(query_tile, tile_id, doc_tile, gate_pad, query_gain, head_count, head_dim):
    row_count = query_tile.shape[0]
    scale_factor = head_dim ** (-0.5)
    normed = norm_rows(
        query_tile.reshape(row_count, head_count, head_dim), query_gain, scale_factor
    ).astype(jnp.bfloat16)
    query_rows = normed.transpose(1, 0, 2).reshape(head_count * row_count, head_dim)
    tile_first = tile_id * row_count
    doc_first = doc_tile * row_count
    query_gate = lax.dynamic_slice_in_dim(gate_pad, tile_first, row_count, 1)
    block_count = (tile_first + row_count - doc_first + key_span - 1) // key_span
    return (query_rows, tile_first, doc_first, query_gate, block_count)


def forward_task(
    query_tile, tile_id, doc_tile, key_pad, value_pad, gate_pad, query_gain, head_count
):
    row_count, full_width = query_tile.shape
    head_dim = key_pad.shape[1]
    query_rows, tile_first, doc_first, query_gate, block_count = query_setup(
        query_tile, tile_id, doc_tile, gate_pad, query_gain, head_count, head_dim
    )

    def block_step(block_index, loop_state):
        row_total, value_sum = loop_state
        block_first = doc_first + block_index * key_span
        scores, key_block = block_scores(
            query_rows,
            key_pad,
            gate_pad,
            query_gate,
            block_first,
            tile_first,
            doc_first,
            head_count,
        )
        weights = jnp.exp(scores)
        value_block = lax.dynamic_slice_in_dim(value_pad, block_first, key_span, 0)
        mixed_rows = jnp.dot(
            weights.reshape(head_count * row_count, key_span).astype(jnp.bfloat16),
            value_block,
            preferred_element_type=jnp.float32,
        )
        return (row_total + jnp.sum(weights, axis=2), value_sum + mixed_rows)

    start_state = (
        jnp.zeros((head_count, row_count), jnp.float32),
        jnp.zeros((head_count * row_count, head_dim), jnp.float32),
    )
    row_total, value_sum = lax.fori_loop(0, block_count, block_step, start_state)
    result = value_sum.reshape(head_count, row_count, head_dim) / row_total[:, :, None]
    return result.transpose(1, 0, 2).reshape(row_count, full_width).astype(jnp.bfloat16)


def backward_task(
    partials,
    query_tile,
    grad_tile,
    out_tile,
    tile_id,
    doc_tile,
    key_pad,
    value_pad,
    gate_pad,
    query_gain,
    head_count,
):
    row_count, full_width = query_tile.shape
    head_dim = key_pad.shape[1]
    query_rows, tile_first, doc_first, query_gate, block_count = query_setup(
        query_tile, tile_id, doc_tile, gate_pad, query_gain, head_count, head_dim
    )
    grad_rows = (
        grad_tile.reshape(row_count, head_count, head_dim)
        .transpose(1, 0, 2)
        .reshape(head_count * row_count, head_dim)
    )
    product = grad_tile.astype(jnp.float32) * out_tile.astype(jnp.float32)
    out_inner = jnp.sum(product.reshape(row_count, head_count, head_dim), axis=2).T

    def total_step(block_index, row_total):
        block_first = doc_first + block_index * key_span
        scores, key_block = block_scores(
            query_rows,
            key_pad,
            gate_pad,
            query_gate,
            block_first,
            tile_first,
            doc_first,
            head_count,
        )
        return row_total + jnp.sum(jnp.exp(scores), axis=2)

    row_total = lax.fori_loop(
        0, block_count, total_step, jnp.zeros((head_count, row_count), jnp.float32)
    )

    def grad_step(block_index, loop_state):
        key_part, value_part, gate_part, query_grad, row_sum = loop_state
        block_first = doc_first + block_index * key_span
        scores, key_block = block_scores(
            query_rows,
            key_pad,
            gate_pad,
            query_gate,
            block_first,
            tile_first,
            doc_first,
            head_count,
        )
        probability = jnp.exp(scores) / row_total[:, :, None]
        value_block = lax.dynamic_slice_in_dim(value_pad, block_first, key_span, 0)
        prob_grad = contract_last(grad_rows, value_block).reshape(head_count, row_count, key_span)
        score_grad = probability * (prob_grad - out_inner[:, :, None])
        score_low = score_grad.reshape(head_count * row_count, key_span).astype(jnp.bfloat16)
        prob_low = probability.reshape(head_count * row_count, key_span).astype(jnp.bfloat16)
        query_grad = query_grad + jnp.dot(score_low, key_block, preferred_element_type=jnp.float32)
        key_update = contract_first(score_low, query_rows)
        value_update = contract_first(prob_low, grad_rows)
        key_part = lax.dynamic_update_slice_in_dim(
            key_part,
            lax.dynamic_slice_in_dim(key_part, block_first, key_span, 0) + key_update,
            block_first,
            0,
        )
        value_part = lax.dynamic_update_slice_in_dim(
            value_part,
            lax.dynamic_slice_in_dim(value_part, block_first, key_span, 0) + value_update,
            block_first,
            0,
        )
        column_sum = jnp.sum(score_grad, axis=1)
        gate_part = lax.dynamic_update_slice_in_dim(
            gate_part,
            lax.dynamic_slice_in_dim(gate_part, block_first, key_span, 1) - column_sum,
            block_first,
            1,
        )
        return (key_part, value_part, gate_part, query_grad, row_sum + jnp.sum(score_grad, axis=2))

    start_state = (
        partials[0],
        partials[1],
        partials[2],
        jnp.zeros((head_count * row_count, head_dim), jnp.float32),
        jnp.zeros((head_count, row_count), jnp.float32),
    )
    key_part, value_part, gate_part, query_grad, row_sum = lax.fori_loop(
        0, block_count, grad_step, start_state
    )
    gate_part = lax.dynamic_update_slice_in_dim(
        gate_part,
        lax.dynamic_slice_in_dim(gate_part, tile_first, row_count, 1) + row_sum,
        tile_first,
        1,
    )
    query_result = (
        query_grad.reshape(head_count, row_count, head_dim)
        .transpose(1, 0, 2)
        .reshape(row_count, full_width)
        .astype(jnp.bfloat16)
    )
    return ((key_part, value_part, gate_part), query_result)


def full_reduce(key_rows_all, value_rows_all, suffix):
    return (
        lax.psum_scatter(
            key_rows_all.astype(jnp.bfloat16), "seq", scatter_dimension=0, tiled=True
        ).astype(jnp.float32),
        lax.psum_scatter(
            value_rows_all.astype(jnp.bfloat16), "seq", scatter_dimension=0, tiled=True
        ).astype(jnp.float32),
        lax.psum_scatter(
            suffix.astype(jnp.bfloat16), "seq", scatter_dimension=1, tiled=True
        ).astype(jnp.float32),
    )


def on_device(queries, key_vectors, values, forget_logit, out_grad, query_gain, key_gain, lengths):
    query_local = queries[0]
    key_local = key_vectors[0]
    value_local = values[0]
    logit_local = forget_logit[0]
    grad_local = out_grad[0]
    row_count, full_width = query_local.shape
    head_dim = key_local.shape[1]
    head_count = full_width // head_dim
    tile_dev = row_count // TILE
    servers = lax.axis_size("seq")
    owner_index = lax.axis_index("seq")
    tile_count = servers * tile_dev
    token_count = tile_count * TILE
    starts = tile_starts(lengths[0], tile_count)
    key_normed = norm_rows(key_local, key_gain, 1.0).astype(jnp.bfloat16)
    pads = prepare(
        (
            lax.all_gather(key_normed, "seq", axis=0, tiled=True),
            lax.all_gather(value_local, "seq", axis=0, tiled=True),
            lax.all_gather(logit_local, "seq", axis=1, tiled=True),
        )
    )
    lane_index = jnp.arange(tile_dev, dtype=jnp.int32)
    own_ids = owner_index * tile_dev + lane_index
    query_tiles = query_local.reshape(tile_dev, TILE, full_width)
    grad_tiles = grad_local.reshape(tile_dev, TILE, full_width)
    pad_set = pads
    out_tiles = lax.map(
        lambda task_item: forward_task(
            task_item[0],
            task_item[1],
            starts[task_item[1]],
            pad_set[0],
            pad_set[1],
            pad_set[2],
            query_gain,
            head_count,
        ),
        (query_tiles, own_ids),
    )
    pads = prepare(
        (
            lax.all_gather(key_normed, "seq", axis=0, tiled=True),
            lax.all_gather(value_local, "seq", axis=0, tiled=True),
            lax.all_gather(logit_local, "seq", axis=1, tiled=True),
        )
    )
    run_pad_set = pads
    zero_parts = (
        jnp.zeros(run_pad_set[0].shape, jnp.float32),
        jnp.zeros(run_pad_set[1].shape, jnp.float32),
        jnp.zeros(run_pad_set[2].shape, jnp.float32),
    )

    def task_step(partials, task_item):
        query_tile, grad_tile, out_tile, tile_id = task_item
        return backward_task(
            partials,
            query_tile,
            grad_tile,
            out_tile,
            tile_id,
            starts[tile_id],
            run_pad_set[0],
            run_pad_set[1],
            run_pad_set[2],
            query_gain,
            head_count,
        )

    partials, query_grad_tiles = lax.scan(
        task_step, zero_parts, (query_tiles, grad_tiles, out_tiles, own_ids)
    )
    key_part, value_part, gate_part = partials
    suffix = jnp.flip(jnp.cumsum(jnp.flip(gate_part[:, :token_count], 1), axis=1), 1)
    normed_key_grad, value_sum, gate_grad = full_reduce(
        key_part[:token_count], value_part[:token_count], suffix
    )
    _, key_pullback = jax.vjp(
        lambda raw_values, gain_vec: norm_rows(raw_values, gain_vec, 1.0),
        key_local.astype(jnp.float32),
        key_gain,
    )
    key_input_grad, key_gain_part = key_pullback(normed_key_grad)
    scale_factor = head_dim ** (-0.5)
    _, query_pullback = jax.vjp(
        lambda raw_values, gain_vec: norm_rows(raw_values, gain_vec, scale_factor),
        query_local.reshape(row_count, head_count, head_dim).astype(jnp.float32),
        query_gain,
    )
    query_input_grad, query_gain_part = query_pullback(
        query_grad_tiles.reshape(row_count, head_count, head_dim).astype(jnp.float32)
    )
    forget_grad = gate_grad * jax.nn.sigmoid(-logit_local.astype(jnp.float32))
    gain_total = lax.psum(jnp.stack([query_gain_part, key_gain_part]), ("seq", "rep"))
    attention = out_tiles.reshape(row_count, full_width)
    return (
        attention[None],
        query_input_grad.reshape(row_count, full_width).astype(jnp.bfloat16)[None],
        key_input_grad.astype(jnp.bfloat16)[None],
        value_sum.astype(jnp.bfloat16)[None],
        forget_grad[None],
        gain_total,
    )


def solution(mesh):
    return jax.shard_map(
        on_device,
        mesh=mesh,
        in_specs=(
            P("rep", "seq", None),
            P("rep", "seq", None),
            P("rep", "seq", None),
            P("rep", None, "seq"),
            P("rep", "seq", None),
            P(),
            P(),
            P("rep", None),
        ),
        out_specs=(
            P("rep", "seq", None),
            P("rep", "seq", None),
            P("rep", "seq", None),
            P("rep", "seq", None),
            P("rep", None, "seq"),
            P(),
        ),
        check_vma=False,
    )
```

profile of v0, /device:TPU:0, one launch (start us, length us, event | category | flops | bytes accessed | tf_op | source)
XLA Modules:
  0.0 1158.8 jit_solution(2210623422590309497)
XLA Ops:
  8.9 1.6 fusion.42
  10.6 25.7 %all-gather = bf16[1,4,8192]{2,1,0:T(4,128)(2,1)S(1)} all-gather(bf16[1,4,256]{2,1,0:T(4,128)(2,1)} %param.21), channel_id=2, replica_groups=mesh['seq'=32,'rep'=4] {'seq'}, dimensions={2}, use_global_device_ids=true | all-gather | bytes 67584 | tf_op jit(solution)/shard_map/all_gather | solution.py:265
  36.5 1.2 reduce-window.24
  40.6 16.1 %all-gather.7.cloned.1.call-done = bf16[1,8192,128]{2,1,0:T(8,128)(2,1)} async-done(((bf16[1,256,128]{2,1,0:T(8,128)(2,1)}), bf16[1,8192,128]{2,1,0:T(8,128)(2,1)}) %all-gather.7.cloned.1.call-update) | async-done | bytes 2097168 | tf_op jit(solution)/shard_map/all_gather | solution.py:264
  56.8 2.8 pad.16
  59.6 43.3 %all-gather.5.cloned.1.call-done = bf16[8192,128]{1,0:T(8,128)(2,1)} async-done(((bf16[256,128]{1,0:T(8,128)(2,1)}), bf16[8192,128]{1,0:T(8,128)(2,1)}) %all-gather.5.cloned.1.call-update) | async-done | bytes 2097168 | tf_op jit(solution)/shard_map/all_gather | solution.py:263
  102.9 1.7 pad.15
  105.3 42.2 %while.166 = (s32[]{:T(128)}, bf16[4,64,512]{2,1,0:T(8,128)(2,1)}, s32[4]{0:T(128)S(1)}, s32[128]{0:T(128)S(1)}, bf16[4,64,512]{2,1,0:T(8,128)(2,1)}, /*index=5*...) while((s32[]{:T(128)}, bf16[4,64,512]{2,1,0:T(8,128)(2,1)}, ...), condition=%wide.region_10.11_spmd, body=%wide.region_5.10_spmd.sunk | while | flops 68126688 | bytes 5365146 | solution.py:273
  111.8 3.1 while.170
  113.6 1.2 convolution_add_fusion.11
  122.4 3.1 while.170
  124.2 1.2 convolution_add_fusion.11
  132.9 3.1 while.170
  134.7 1.2 convolution_add_fusion.11
  143.5 3.1 while.170
  145.3 1.2 convolution_add_fusion.11
  147.5 2.2 broadcast.429
  149.7 2.2 broadcast.429.clone
  153.3 92.5 %while.169 = (s32[]{:T(128)}, f32[8704,128]{1,0:T(8,128)}, f32[8704,128]{1,0:T(8,128)}, f32[4,8704]{1,0:T(4,128)}, bf16[4,64,512]{2,1,0:T(8,128)(2,1)}, /*index=...) while((s32[]{:T(128)}, f32[8704,128]{1,0:T(8,128)}, ...), condition=%wide.region_21.22_spmd, body=%wide.region_11.21_spmd.sunk | while | flops 204607008 | bytes 11736533 | solution.py:316
  159.9 1.9 while.171
  163.9 9.7 while.172
  165.1 1.3 fusion.130
  166.4 1.9 fusion.132
  168.3 1.9 fusion.131
  170.2 1.0 multiply_reduce_fusion.14
  171.9 1.3 dynamic_update_slice.58
  175.1 1.3 dynamic_update_slice.55
  183.0 1.9 while.171
  187.0 9.7 while.172
  188.2 1.3 fusion.130
  189.5 1.9 fusion.132
  191.4 1.9 fusion.131
  193.3 1.0 multiply_reduce_fusion.14
  195.1 1.3 dynamic_update_slice.58
  198.3 1.4 dynamic_update_slice.55
  206.2 1.9 while.171
  210.2 9.7 while.172
  211.4 1.3 fusion.130
  212.7 1.9 fusion.132
  214.6 1.9 fusion.131
  216.5 1.0 multiply_reduce_fusion.14
  218.3 1.3 dynamic_update_slice.58
  221.4 1.3 dynamic_update_slice.55
  229.2 1.9 while.171
  233.2 9.7 while.172
  234.4 1.3 fusion.130
  235.7 1.9 fusion.132
  237.6 1.9 fusion.131
  241.2 1.3 dynamic_update_slice.58
  244.4 1.4 dynamic_update_slice.55
  246.7 5.6 rev.7
  252.3 1.2 reduce-window.31
  254.1 5.8 rev.8
  259.8 1.9 copy.100
  261.8 3.8 slice.39
  265.6 3.7 slice.38
  269.4 1.1 reshape.574
  273.0 1.9 fusion.39
  274.9 713.4 %reduce-scatter.10.cloned.1.call-done = bf16[256,4]{1,0:T(8,128)(2,1)} async-done(((bf16[8192,4]{1,0:T(8,128)(2,1)}), bf16[256,4]{1,0:T(8,128)(2,1)}) %reduce-scatter.10.cloned.1.call-update) | async-done | bytes 2064
  989.9 80.1 %reduce-scatter.6.cloned.1.call-done = bf16[256,128]{1,0:T(8,128)(2,1)} async-done(((bf16[8192,128]{1,0:T(8,128)(2,1)}), bf16[256,128]{1,0:T(8,128)(2,1)}) %reduce-scatter.6.cloned.1.call-update) | async-done | bytes 65552 | tf_op jit(solution)/shard_map/reduce_scatter | solution.py:233
  1070.0 1.0 fusion.43
  1071.0 64.8 %psum.7 = f32[2,128]{1,0:T(2,128)} all-reduce(f32[2,128]{1,0:T(2,128)S(1)} %pad_maximum_fusion), channel_id=1, replica_groups=mesh['seq'=32,'rep'=4] {'seq','rep'}, use_global_device_ids=true, to_apply=%region_33.34 | all-reduce | flops 256 | bytes 2048 | tf_op jit(solution)/shard_map/psum | solution.py:340
  1135.9 1.6 fusion.53
  1137.5 14.7 %reduce-scatter.8.cloned.1.call-done = bf16[256,128]{1,0:T(8,128)(2,1)} async-done(((bf16[8192,128]{1,0:T(8,128)(2,1)}), bf16[256,128]{1,0:T(8,128)(2,1)}) %reduce-scatter.8.cloned.1.call-update) | async-done | bytes 65552 | tf_op jit(solution)/shard_map/reduce_scatter | solution.py:236
  (394 shorter events, 80.3 us)
Async XLA Ops:
  7.2 49.6 %all-gather.7.cloned.1.call-start = ((), (), s32[]{:S(2)}) async-start(), calls=%async_computation.6 | async-start | bytes 2162688 | tf_op jit(solution)/shard_map/all_gather | solution.py:264
  7.9 95.0 %all-gather.5.cloned.1.call-start = ((), (), s32[]{:S(2)}) async-start(), calls=%async_computation.3 | async-start | bytes 2162688 | tf_op jit(solution)/shard_map/all_gather | solution.py:263
  10.5 977.8 %reduce-scatter.10.cloned.1.call-start = ((), (), s32[]{:S(2)}) async-start(), calls=%async_computation.7 | async-start | bytes 2162688
  56.8 48.5 %copy-start.6 = (f32[128]{0:T(128)S(1)}, f32[128]{0:T(128)}, u32[]{:S(2)}) copy-start(f32[128]{0:T(128)} %param.23) | copy-start | bytes 1540
  110.5 1.4 copy-start.3
  121.0 1.4 copy-start.3
  131.6 1.4 copy-start.3
  142.1 1.4 copy-start.3
  158.5 1.4 copy-start
  181.6 1.4 copy-start
  204.8 1.4 copy-start
  227.8 1.4 copy-start
  261.7 808.3 %reduce-scatter.6.cloned.1.call-start = ((), (), s32[]{:S(2)}) async-start(), calls=%async_computation.4 | async-start | bytes 2162688 | tf_op jit(solution)/shard_map/reduce_scatter | solution.py:233
  265.5 5.0 copy-start.1
  265.6 886.7 %reduce-scatter.8.cloned.1.call-start = ((), (), s32[]{:S(2)}) async-start(), calls=%async_computation.5 | async-start | bytes 2162688 | tf_op jit(solution)/shard_map/reduce_scatter | solution.py:236
  270.5 718.7 %copy-start.4 = (bf16[1,4,256]{2,1,0:T(4,128)(2,1)S(1)}, bf16[1,4,256]{2,1,0:T(4,128)(2,1)}, u32[]{:S(2)}) copy-start(bf16[1,4,256]{2,1,0:T(4,128)(2,1)} %param.21) | copy-start | bytes 6148
  270.5 799.5 %copy-start.2 = (bf16[1,256,128]{2,1,0:T(8,128)(2,1)S(1)}, bf16[1,256,128]{2,1,0:T(8,128)(2,1)}, u32[]{:S(2)}) copy-start(bf16[1,256,128]{2,1,0:T(8,128)(2,1)} %param.19) | copy-start | bytes 196612
  270.6 799.5 %copy-start.5 = (f32[128]{0:T(128)S(1)}, f32[128]{0:T(128)}, u32[]{:S(2)}) copy-start(f32[128]{0:T(128)} %param.24) | copy-start | bytes 1540
Sparse Core Ops, SparseCore 0:
  10.3 46.4 all-gather.6
  59.6 43.2 all-gather.4
  261.8 726.4 reduce-scatter.9
  991.7 78.2 reduce-scatter.5
  1074.0 78.2 reduce-scatter.7
where the time goes:
time: 1180 us; the launch traced here: 1160 us
  waiting for transfers between devices  868 us (74%)
  local copies, waits for them, and re-layouts  92.9 us (8%)
  blocking collectives  90.6 us (8%)
  other arithmetic  34.9 us (3%)
  matrix products  29.6 us (3%)
  loops' own time  28.1 us (2%)
  between operations  14 us (1%)
    unnamed x6, waiting for transfers between devices  714 us
    reduce_scatter x1, waiting for transfers between devices, full_reduce(): lax.psum_scatter(key_rows_all.astype(jnp.bfloat16), 'seq', scatter_dimens...  80.1 us
    psum x1, blocking collectives, on_device(): lax.psum(jnp.stack([query_gain_part, key_gain_part]), ('seq', 'rep'))  64.8 us
    all_gather x1, waiting for transfers between devices, on_device(): lax.all_gather(key_normed, 'seq', axis=0, tiled=True)  43.3 us
    all_gather x1, blocking collectives, on_device(): lax.all_gather(logit_local, 'seq', axis=1, tiled=True)  25.7 us
  transfers between devices with their start and end apart: 5, of which 5 were waited for; matrix products, arithmetic and copies ran while one was open for 2% of the time, Pallas kernels for 0%

commit v1 on v0

v1 whole, which is shorter than its diff:
```python
import functools
import math

import jax
import jax.numpy as jnp
from jax import lax
from jax.experimental import pallas as pl
from jax.experimental.pallas import tpu as pltpu
from jax.sharding import PartitionSpec as P

MESH = pl.DeviceIdType.MESH
F32 = jnp.float32
BF16 = jnp.bfloat16

EPS = 1e-06
HEADS = 4
DH = 128
TOK = 256
TILE = 64
SHARDS = 32
HEAD_ROWS = 16
ROWS = HEAD_ROWS + TOK
PIECES = ((0, 80), (80, 144), (144, 208), (208, 272))
LOG2E = math.log2(math.e)
LN2 = math.log(2.0)
FAR = (2, -1, 1, 0)


def spot():
    me = lax.axis_index("seq")
    return me // 8, (me // 2) % 4, me % 2


def shard_at(tree, da, db, core=None):
    z, y, c = spot()
    dz, dy = (da, db) if tree == 0 else (db, da)
    c = c if core is None else core
    return (((z + dz + 4) % 4) * 4 + (y + dy + 4) % 4) * 2 + c


def cell_at(tree, da, db):
    z, y, _ = spot()
    dz, dy = (da, db) if tree == 0 else (db, da)
    return ((z + dz + 4) % 4) * 4 + (y + dy + 4) % 4


def piece(tree, part):
    low, high = PIECES[2 * tree], PIECES[2 * tree + 1]
    first, last = {"a": low, "b": high, "ab": (low[0], high[1])}[part]
    return first, last - first


def rows_of(tree, part):
    first, count = piece(tree, part)
    return pl.ds(first, count)


def greet(devices):
    barrier = pltpu.get_barrier_semaphore()
    for device in devices:
        pl.semaphore_signal(barrier, inc=1, device_id=device, device_id_type=MESH)
    pl.semaphore_wait(barrier, len(devices))


def neighbours():
    found = [{"seq": shard_at(tree, step, 0)} for tree in (0, 1) for step in (1, -1)]
    return found + [{"seq": shard_at(0, 0, 0, 1 - spot()[2])}]


def ring_events():
    names = ["A-", "A+", "A2a", "A2b"]
    for da in FAR:
        names += [("B-", da), ("B+", da), ("B2a", da), ("B2b", da)]
    return names


def split3(x):
    high = x.astype(BF16)
    rest = x - high.astype(F32)
    mid = rest.astype(BF16)
    low = (rest - mid.astype(F32)).astype(BF16)
    return high, mid, low


def gather_kernel(key_ref, value_ref, logit_ref, gain_ref, out_ref, mine, send_sem, recv_sem, own_sem):
    greet(neighbours())
    me = lax.axis_index("seq")
    sibling = {"seq": shard_at(0, 0, 0, 1 - spot()[2])}

    raw = key_ref[...].astype(F32)
    scale = lax.rsqrt(jnp.mean(raw * raw, axis=1, keepdims=True) + EPS)
    mine[HEAD_ROWS:, 0:DH] = (raw * scale * gain_ref[...]).astype(BF16)
    mine[HEAD_ROWS:, DH:] = value_ref[...]
    logit = logit_ref[...].astype(F32)
    decay = jnp.minimum(logit, 0.0) - jnp.log1p(jnp.exp(-jnp.abs(logit)))
    row = lax.broadcasted_iota(jnp.int32, (TOK, TOK), 0)
    column = lax.broadcasted_iota(jnp.int32, (TOK, TOK), 1)
    upper = (row <= column).astype(F32)
    local = jnp.dot(decay, upper, preferred_element_type=F32, precision=lax.Precision.HIGHEST)
    high = local.astype(BF16).astype(F32)
    mid = (local - high).astype(BF16).astype(F32)
    low = local - high - mid
    zero = jnp.zeros((4, TOK), F32)
    mine[0:HEAD_ROWS, :] = jnp.concatenate([high, mid, low, zero], axis=0).astype(BF16)

    ids = {}
    for tree in (0, 1):
        for name in ring_events():
            ids[tree, name] = len(ids)
        for da in FAR:
            for db in FAR:
                ids[tree, "D", da, db] = len(ids)
    started = []

    def copy(event, source, place, rows, device):
        number = ids[event]
        made = pltpu.make_async_remote_copy(
            src_ref=source.at[rows],
            dst_ref=out_ref.at[place, rows],
            send_sem=send_sem.at[number],
            recv_sem=recv_sem.at[number],
            device_id=device,
            device_id_type=MESH,
        )
        made.start()
        started.append(made)

    def arrived(event, place, rows):
        number = ids[event]
        part = out_ref.at[place, rows]
        pltpu.make_async_remote_copy(
            src_ref=part,
            dst_ref=part,
            send_sem=send_sem.at[number],
            recv_sem=recv_sem.at[number],
            device_id=sibling,
            device_id_type=MESH,
        ).wait_recv()

    def send(event, tree, da, db, part, target):
        place = shard_at(tree, da, db)
        source = mine if (da, db) == (0, 0) else out_ref.at[place]
        device = {"seq": shard_at(tree, *target)}
        copy(event, source, place, rows_of(tree, part), device)

    def share(tree, da, db):
        place = shard_at(tree, da, db)
        source = mine if (da, db) == (0, 0) else out_ref.at[place]
        copy((tree, "D", da, db), source, place, rows_of(tree, "ab"), sibling)

    def wait(tree, name, da, db, part):
        arrived((tree, name), shard_at(tree, da, db), rows_of(tree, part))

    for tree in (0, 1):
        send((tree, "A-"), tree, 0, 0, "ab", (1, 0))
        send((tree, "A+"), tree, 0, 0, "ab", (-1, 0))
    own = pltpu.make_async_copy(mine, out_ref.at[me], own_sem)
    own.start()
    for tree in (0, 1):
        send((tree, ("B-", 0)), tree, 0, 0, "ab", (0, 1))
        send((tree, ("B+", 0)), tree, 0, 0, "ab", (0, -1))
        share(tree, 0, 0)

    for tree in (0, 1):
        wait(tree, "A-", -1, 0, "ab")
        send((tree, "A2a"), tree, -1, 0, "a", (1, 0))
        wait(tree, "A+", 1, 0, "ab")
        send((tree, "A2b"), tree, 1, 0, "b", (-1, 0))
        for da in (-1, 1):
            send((tree, ("B-", da)), tree, da, 0, "ab", (0, 1))
            send((tree, ("B+", da)), tree, da, 0, "ab", (0, -1))
            share(tree, da, 0)

    def near(tree, da):
        wait(tree, ("B-", da), da, -1, "ab")
        send((tree, ("B2a", da)), tree, da, -1, "a", (0, 1))
        wait(tree, ("B+", da), da, 1, "ab")
        send((tree, ("B2b", da)), tree, da, 1, "b", (0, -1))
        share(tree, da, -1)
        share(tree, da, 1)

    def far(tree, da):
        wait(tree, ("B2a", da), da, 2, "a")
        wait(tree, ("B2b", da), da, 2, "b")
        share(tree, da, 2)

    for tree in (0, 1):
        near(tree, 0)
    for tree in (0, 1):
        wait(tree, "A2a", 2, 0, "a")
        wait(tree, "A2b", 2, 0, "b")
        send((tree, ("B-", 2)), tree, 2, 0, "ab", (0, 1))
        send((tree, ("B+", 2)), tree, 2, 0, "ab", (0, -1))
        share(tree, 2, 0)
    for da in (-1, 1):
        for tree in (0, 1):
            near(tree, da)
    for tree in (0, 1):
        far(tree, 0)
    for tree in (0, 1):
        near(tree, 2)
    for da in (-1, 1, 2):
        for tree in (0, 1):
            far(tree, da)
    other = 1 - spot()[2]
    for tree in (0, 1):
        for da in FAR:
            for db in FAR:
                arrived((tree, "D", da, db), shard_at(tree, da, db, other), rows_of(tree, "ab"))
    for made in started:
        made.wait_send()
    own.wait()


EVENTS = 2 * (20 + 16)


def gather(key_local, value_local, logit_local, key_gain):
    vmem = pl.BlockSpec(memory_space=pltpu.VMEM)
    return pl.pallas_call(
        gather_kernel,
        out_shape=jax.ShapeDtypeStruct((SHARDS, ROWS, 2 * DH), BF16),
        in_specs=[vmem] * 4,
        out_specs=pl.BlockSpec(memory_space=pl.ANY),
        scratch_shapes=[
            pltpu.VMEM((ROWS, 2 * DH), BF16),
            pltpu.SemaphoreType.DMA((EVENTS,)),
            pltpu.SemaphoreType.DMA((EVENTS,)),
            pltpu.SemaphoreType.DMA(()),
        ],
        compiler_params=pltpu.CompilerParams(collective_id=0, has_side_effects=True),
        name="gather_shards",
    )(key_local, value_local, logit_local, key_gain)


def row_to_columns(row):
    parts = [
        jnp.transpose(jnp.broadcast_to(row[:, half * DH : (half + 1) * DH], (DH, DH)))
        for half in (0, 1)
    ]
    return jnp.concatenate(parts, axis=0)


def split_lanes(full):
    high, mid, low = split3(full)
    lane = lax.broadcasted_iota(jnp.int32, full.shape, 1)
    picked = jnp.where(
        lane == 0,
        high.astype(F32),
        jnp.where(lane == 1, mid.astype(F32), jnp.where(lane == 2, low.astype(F32), 0.0)),
    )
    return picked.astype(BF16)


def contract_last(left, right):
    return lax.dot_general(left, right, (((1,), (1,)), ((), ())), preferred_element_type=F32)


def contract_first(left, right):
    return lax.dot_general(left, right, (((0,), (0,)), ((), ())), preferred_element_type=F32)


def attend_kernel(
    place_ref,
    length_ref,
    kv_ref,
    query_ref,
    grad_ref,
    query_gain_ref,
    key_gain_ref,
    att_ref,
    query_grad_ref,
    part_ref,
    gain_ref,
    gate,
    query_wide,
    query_low,
    grad_wide,
    grad_low,
    prob,
    score_low,
    out_sum,
    column,
    key_gain_sum,
):
    me = place_ref[0]
    ones = jnp.ones((TOK, DH), BF16)

    starts = []
    for tile in range(TOK // TILE):
        at = me * (TOK // TILE) + tile
        end = jnp.int32(0)
        start = jnp.int32(0)
        for document in range(4):
            end = end + length_ref[document]
            start = jnp.where(end <= at, end, start)
        starts.append(start * TILE)
    low_block = starts[0] // TOK

    carry = jnp.zeros((4, DH), F32)
    for shard in range(SHARDS):
        packed = kv_ref[shard, 0:HEAD_ROWS, :].astype(F32)
        local = (packed[0:4] + packed[4:8] + packed[8:12]) * LOG2E
        gate[shard, 0:4, :] = local + jnp.concatenate([carry, carry], axis=1)
        carry = carry + jnp.broadcast_to(local[:, TOK - 1 :], (4, DH))

    query_scale = query_gain_ref[...] * (DH**-0.5)
    for head in range(HEADS):
        raw = query_ref[:, head * DH : (head + 1) * DH].astype(F32)
        scale = lax.rsqrt(jnp.mean(raw * raw, axis=1, keepdims=True) + EPS)
        normed = (raw * scale * (query_scale * LOG2E)).astype(BF16)
        own_gate = row_to_columns(gate[me, head : head + 1, :])
        query_low[head * TOK : (head + 1) * TOK, :] = normed
        query_wide[head] = jnp.concatenate([normed, split_lanes(own_gate)], axis=1)
    out_sum[...] = jnp.zeros_like(out_sum)
    column[...] = jnp.zeros_like(column)
    key_gain_sum[...] = jnp.zeros_like(key_gain_sum)

    lane_token = lax.broadcasted_iota(jnp.int32, (1, TOK), 1)

    def forward_block(block, diagonal):
        keys = kv_ref[block, HEAD_ROWS:, 0:DH]
        values = kv_ref[block, HEAD_ROWS:, DH:]
        key_wide = jnp.concatenate([keys, ones], axis=1)
        value_wide = jnp.concatenate([values, ones], axis=1)
        token = block * TOK + lane_token
        for head in range(HEADS):
            scores = contract_last(query_wide[head], key_wide)
            key_gate = gate[block, head : head + 1, :]
            pieces = []
            for tile in range(TOK // TILE):
                low = jnp.where(token >= starts[tile], key_gate, jnp.inf)
                pieces.append(scores[tile * TILE : (tile + 1) * TILE] - low)
            scores = jnp.concatenate(pieces, axis=0)
            if diagonal:
                row = lax.broadcasted_iota(jnp.int32, (TOK, TOK), 0)
                col = lax.broadcasted_iota(jnp.int32, (TOK, TOK), 1)
                scores = jnp.where(col <= row, scores, -jnp.inf)
            weights = jnp.exp2(scores).astype(BF16)
            prob[block, head * TOK : (head + 1) * TOK, :] = weights
            out_sum[head] += jnp.dot(weights, value_wide, preferred_element_type=F32)

    def forward_step(block, _):
        forward_block(block, False)
        return 0

    lax.fori_loop(low_block, me, forward_step, 0)
    forward_block(me, True)

    for head in range(HEADS):
        span = slice(head * DH, (head + 1) * DH)
        inverse = 1.0 / out_sum[head, :, DH:]
        out = out_sum[head, :, 0:DH] * inverse
        att_ref[:, span] = out.astype(BF16)
        scaled = (grad_ref[:, span].astype(F32) * inverse).astype(BF16)
        inner = jnp.sum(scaled.astype(F32) * out, axis=1, keepdims=True)
        grad_low[head * TOK : (head + 1) * TOK, :] = scaled
        grad_wide[head] = jnp.concatenate(
            [scaled, split_lanes(jnp.broadcast_to(-inner, (TOK, DH)))], axis=1
        )
    out_sum[...] = jnp.zeros_like(out_sum)

    def clear_step(block, _):
        part_ref[block] = jnp.zeros((ROWS, 2 * DH), BF16)
        return 0

    lax.fori_loop(0, low_block, clear_step, 0)
    lax.fori_loop(me + 1, SHARDS, clear_step, 0)

    def backward_step(block, _):
        keys = kv_ref[block, HEAD_ROWS:, 0:DH]
        values = kv_ref[block, HEAD_ROWS:, DH:]
        key_wide = jnp.concatenate([keys, ones], axis=1)
        value_wide = jnp.concatenate([values, ones], axis=1)
        for head in range(HEADS):
            span = slice(head * TOK, (head + 1) * TOK)
            prob_grad = contract_last(grad_wide[head], value_wide)
            score_grad = prob[block, span, :].astype(F32) * prob_grad
            low = score_grad.astype(BF16)
            folded = jnp.sum(low.astype(F32).reshape(TOK // 8, 8, TOK), axis=0)
            column[block, head : head + 1, :] = -jnp.sum(folded, axis=0, keepdims=True)
            score_low[span, :] = low
            out_sum[head] += jnp.dot(low, key_wide, preferred_element_type=F32)
        key_part = contract_first(score_low[...], query_low[...]) * LN2
        value_part = contract_first(prob[block], grad_low[...])
        part_ref[block, HEAD_ROWS:, 0:DH] = key_part.astype(BF16)
        part_ref[block, HEAD_ROWS:, DH:] = value_part.astype(BF16)
        moved = (key_part * keys.astype(F32)).reshape(TOK // 8, 8, DH)
        key_gain_sum[...] += jnp.sum(moved, axis=0)
        return 0

    lax.fori_loop(low_block, me + 1, backward_step, 0)

    query_gain_sum = jnp.zeros((1, DH), F32)
    for head in range(HEADS):
        span = slice(head * DH, (head + 1) * DH)
        raw = query_ref[:, span].astype(F32)
        scale = lax.rsqrt(jnp.mean(raw * raw, axis=1, keepdims=True) + EPS)
        hat = raw * scale
        cotangent = out_sum[head, :, 0:DH]
        query_gain_sum += jnp.sum(cotangent * hat, axis=0, keepdims=True)
        inner = cotangent * query_scale
        mean = jnp.mean(inner * hat, axis=1, keepdims=True)
        query_grad_ref[:, span] = (scale * (inner - hat * mean)).astype(BF16)
        for half in (0, 1):
            tokens = slice(half * DH, (half + 1) * DH)
            turned = jnp.transpose(out_sum[head, tokens, DH:])
            column[me, head : head + 1, tokens] += turned[0:1]
    query_gain_sum = query_gain_sum * (DH**-0.5)
    key_gain_row = jnp.sum(key_gain_sum[...], axis=0, keepdims=True) / key_gain_ref[...]
    gain_ref[...] = jnp.concatenate([query_gain_sum, key_gain_row, jnp.zeros((6, DH), F32)], axis=0)

    carry = jnp.zeros((8, 1), F32)
    last = lax.broadcasted_iota(jnp.int32, (8, TOK), 1) == TOK - 1
    for shard in range(SHARDS - 1, -1, -1):
        local = column[shard]
        whole = local + jnp.where(last, jnp.broadcast_to(carry, (8, TOK)), 0.0)
        high = whole.astype(BF16).astype(F32)
        part_ref[shard, 0:HEAD_ROWS, :] = jnp.concatenate([high, whole - high], axis=0).astype(BF16)
        carry = carry + jnp.sum(local, axis=1, keepdims=True)


def attend(place, lengths_row, shards, query_local, grad_local, query_gain, key_gain):
    vmem = pl.BlockSpec(memory_space=pltpu.VMEM)
    smem = pl.BlockSpec(memory_space=pltpu.SMEM)
    wide = jax.ShapeDtypeStruct((TOK, HEADS * DH), BF16)
    rows = HEADS * TOK
    return pl.pallas_call(
        attend_kernel,
        out_shape=(
            wide,
            wide,
            jax.ShapeDtypeStruct((SHARDS, ROWS, 2 * DH), BF16),
            jax.ShapeDtypeStruct((8, DH), F32),
        ),
        in_specs=[smem, smem] + [vmem] * 5,
        out_specs=(vmem,) * 4,
        scratch_shapes=[
            pltpu.VMEM((SHARDS, 8, TOK), F32),
            pltpu.VMEM((HEADS, TOK, 2 * DH), BF16),
            pltpu.VMEM((rows, DH), BF16),
            pltpu.VMEM((HEADS, TOK, 2 * DH), BF16),
            pltpu.VMEM((rows, DH), BF16),
            pltpu.VMEM((SHARDS, rows, TOK), BF16),
            pltpu.VMEM((rows, TOK), BF16),
            pltpu.VMEM((HEADS, TOK, 2 * DH), F32),
            pltpu.VMEM((SHARDS, 8, TOK), F32),
            pltpu.VMEM((8, DH), F32),
        ],
        compiler_params=pltpu.CompilerParams(vmem_limit_bytes=56 * 2**20),
        name="attend_both",
    )(place, lengths_row, shards, query_local, grad_local, query_gain, key_gain)


def scatter_kernel(
    part_ref,
    gain_ref,
    key_ref,
    logit_ref,
    key_gain_ref,
    key_grad_ref,
    value_grad_ref,
    forget_grad_ref,
    gain_out_ref,
    twin,
    total,
    landed,
    gain_sum,
    gain_landed,
    send_sem,
    recv_sem,
    gain_send,
    gain_recv,
):
    z, y, core = spot()
    rep = lax.axis_index("rep")
    sibling = {"seq": shard_at(0, 0, 0, 1 - core)}
    partners = []
    partners.append([{"rep": (rep + step) % 4} for step in (1, 2, 3)])
    partners.append([{"seq": shard_at(0, step, 0)} for step in (1, 2, 3)])
    partners.append([{"seq": shard_at(1, step, 0)} for step in (1, 2, 3)])
    partners.append([sibling])
    greet([device for group in partners for device in group])

    ids = {}
    for tree in (0, 1):
        for name in ring_events():
            ids[tree, name] = len(ids)
    slot = dict(ids)
    for tree in (0, 1):
        for da in FAR:
            for db in FAR:
                ids[tree, "D", da, db] = len(ids)
    started = []

    def copy(number, source, target, device):
        made = pltpu.make_async_remote_copy(
            src_ref=source,
            dst_ref=target,
            send_sem=send_sem.at[number],
            recv_sem=recv_sem.at[number],
            device_id=device,
            device_id_type=MESH,
        )
        made.start()
        started.append(made)

    def arrived(number, target):
        pltpu.make_async_remote_copy(
            src_ref=target,
            dst_ref=target,
            send_sem=send_sem.at[number],
            recv_sem=recv_sem.at[number],
            device_id=sibling,
            device_id_type=MESH,
        ).wait_recv()

    def land(tree, name, part):
        first, count = piece(tree, part)
        return landed.at[slot[tree, name], pl.ds(first - piece(tree, "ab")[0], count)]

    def send(event, tree, da, db, part, target):
        source = total.at[cell_at(tree, da, db), rows_of(tree, part)]
        copy(ids[event], source, land(event[0], event[1], part), {"seq": shard_at(tree, *target)})

    def added(tree, part, terms):
        lifted = [term.astype(F32) for term in terms]
        return functools.reduce(lambda a, b: a + b, lifted)

    def store(target, tree, part, whole):
        if tree == 0 and part in ("a", "ab"):
            gates = whole[0:8] + whole[8:16]
            high = gates.astype(BF16).astype(F32)
            whole = jnp.concatenate([high, gates - high, whole[16:]], axis=0)
        target[...] = whole.astype(BF16)

    def wait_twin(tree, da, db, part="ab"):
        place = cell_at(tree, da, db)
        arrived(ids[tree, "D", da, db], twin.at[place, rows_of(tree, "ab")])

    def twins(tree, da, db, part):
        place, rows = cell_at(tree, da, db), rows_of(tree, part)
        return [part_ref[shard_at(tree, da, db), rows, :], twin[place, rows, :]]

    def put(tree, da, db, part, terms):
        store(total.at[cell_at(tree, da, db), rows_of(tree, part)], tree, part, added(tree, part, terms))

    def gain_copies(axis):
        first = 3 * axis
        return [
            pltpu.make_async_remote_copy(
                src_ref=gain_sum.at[axis],
                dst_ref=gain_landed.at[first + i],
                send_sem=gain_send.at[first + i],
                recv_sem=gain_recv.at[first + i],
                device_id=device,
                device_id_type=MESH,
            )
            for i, device in enumerate(partners[axis])
        ]

    def gain_start(axis):
        for made in gain_copies(axis):
            made.start()

    def gain_add(axis):
        whole = gain_sum[axis]
        for i, made in enumerate(gain_copies(axis)):
            made.wait_recv()
            whole = whole + gain_landed[3 * axis + i]
        for made in gain_copies(axis):
            made.wait_send()
        gain_sum[axis + 1] = whole

    gain_sum[0] = gain_ref[...]
    order = [(da, 2) for da in FAR] + [(da, db) for da in FAR for db in (1, -1)] + [(da, 0) for da in FAR]
    for da, db in order:
        for tree in (0, 1):
            rows = rows_of(tree, "ab")
            source = part_ref.at[shard_at(tree, da, db, 1 - core), rows]
            copy(ids[tree, "D", da, db], source, twin.at[cell_at(tree, da, db), rows], sibling)
    gain_start(0)

    for da in FAR:
        for tree in (0, 1):
            wait_twin(tree, da, 2)
            put(tree, da, 2, "ab", twins(tree, da, 2, "ab"))
            send((tree, ("B2a", da)), tree, da, 2, "a", (0, 1))
            send((tree, ("B2b", da)), tree, da, 2, "b", (0, -1))
    gain_add(0)
    gain_start(1)
    for da in FAR:
        for tree in (0, 1):
            for db, name, near, far in ((1, "B2a", "a", "b"), (-1, "B2b", "b", "a")):
                wait_twin(tree, da, db)
                put(tree, da, db, far, twins(tree, da, db, far))
                target = land(tree, (name, da), near)
                arrived(ids[tree, (name, da)], target)
                put(tree, da, db, near, twins(tree, da, db, near) + [target[...]])
                send((tree, ("B-" if db == 1 else "B+", da)), tree, da, db, "ab", (0, db))
    gain_add(1)
    gain_start(2)
    finals = []
    for da in FAR:
        for tree in (0, 1):
            wait_twin(tree, da, 0)
            terms = twins(tree, da, 0, "ab")
            for name in ("B-", "B+"):
                target = land(tree, (name, da), "ab")
                arrived(ids[tree, (name, da)], target)
                terms.append(target[...])
            put(tree, da, 0, "ab", terms)
            here = total.at[cell_at(tree, da, 0)]
            if da == 2:
                send((tree, "A2a"), tree, 2, 0, "a", (1, 0))
                send((tree, "A2b"), tree, 2, 0, "b", (-1, 0))
            if da in (-1, 1):
                name, part = ("A2a", "a") if da == 1 else ("A2b", "b")
                target = land(tree, name, part)
                arrived(ids[tree, name], target)
                rows = rows_of(tree, part)
                put(tree, da, 0, part, [here[rows, :], target[...]])
                send((tree, "A-" if da == 1 else "A+"), tree, da, 0, "ab", (da, 0))
    gain_add(2)
    gain_start(3)
    for tree in (0, 1):
        terms = [total[cell_at(tree, 0, 0), rows_of(tree, "ab"), :]]
        for name in ("A-", "A+"):
            target = land(tree, name, "ab")
            arrived(ids[tree, name], target)
            terms.append(target[...])
        finals.append(added(tree, "ab", terms))
    gain_add(3)

    whole = jnp.concatenate([finals[0][HEAD_ROWS:], finals[1]], axis=0)
    value_grad_ref[...] = whole[:, DH:].astype(BF16)
    cotangent = whole[:, 0:DH]
    raw = key_ref[...].astype(F32)
    scale = lax.rsqrt(jnp.mean(raw * raw, axis=1, keepdims=True) + EPS)
    hat = raw * scale
    inner = cotangent * key_gain_ref[...]
    mean = jnp.mean(inner * hat, axis=1, keepdims=True)
    key_grad_ref[...] = (scale * (inner - hat * mean)).astype(BF16)

    gates = finals[0][0:4] + finals[0][8:12]
    row = lax.broadcasted_iota(jnp.int32, (TOK, TOK), 0)
    col = lax.broadcasted_iota(jnp.int32, (TOK, TOK), 1)
    lower = (row >= col).astype(F32)
    suffix = jnp.dot(gates, lower, preferred_element_type=F32, precision=lax.Precision.HIGHEST)
    logit = logit_ref[...].astype(F32)
    forget_grad_ref[...] = suffix / (1.0 + jnp.exp(logit))
    gain_out_ref[...] = gain_sum[4][0:2]
    for made in started:
        made.wait_send()


def scatter(parts, gains, key_local, logit_local, key_gain):
    vmem = pl.BlockSpec(memory_space=pltpu.VMEM)
    rows = jax.ShapeDtypeStruct((TOK, DH), BF16)
    return pl.pallas_call(
        scatter_kernel,
        out_shape=(
            rows,
            rows,
            jax.ShapeDtypeStruct((HEADS, TOK), F32),
            jax.ShapeDtypeStruct((2, DH), F32),
        ),
        in_specs=[vmem] * 5,
        out_specs=(vmem,) * 4,
        scratch_shapes=[
            pltpu.VMEM((SHARDS // 2, ROWS, 2 * DH), BF16),
            pltpu.VMEM((SHARDS // 2, ROWS, 2 * DH), BF16),
            pltpu.VMEM((40, PIECES[1][1], 2 * DH), BF16),
            pltpu.VMEM((5, 8, DH), F32),
            pltpu.VMEM((10, 8, DH), F32),
            pltpu.SemaphoreType.DMA((EVENTS,)),
            pltpu.SemaphoreType.DMA((EVENTS,)),
            pltpu.SemaphoreType.DMA((10,)),
            pltpu.SemaphoreType.DMA((10,)),
        ],
        compiler_params=pltpu.CompilerParams(
            collective_id=1, has_side_effects=True, vmem_limit_bytes=40 * 2**20
        ),
        name="scatter_sums",
    )(parts, gains, key_local, logit_local, key_gain)


def on_device(queries, key_vectors, values, forget_logit, out_grad, query_gain, key_gain, lengths):
    key_gain = key_gain.reshape(1, DH)
    query_gain = query_gain.reshape(1, DH)
    key_local, logit_local = key_vectors[0], forget_logit[0]
    place = lax.axis_index("seq").astype(jnp.int32).reshape(1)
    shards = gather(key_local, values[0], logit_local, key_gain)
    attention, query_grad, parts, gains = attend(
        place, lengths[0], shards, queries[0], out_grad[0], query_gain, key_gain
    )
    key_grad, value_grad, forget_grad, gain_grad = scatter(
        parts, gains, key_local, logit_local, key_gain
    )
    return (
        attention[None],
        query_grad[None],
        key_grad[None],
        value_grad[None],
        forget_grad[None],
        gain_grad,
    )


def solution(mesh):
    return jax.shard_map(
        on_device,
        mesh=mesh,
        in_specs=(
            P("rep", "seq", None),
            P("rep", "seq", None),
            P("rep", "seq", None),
            P("rep", None, "seq"),
            P("rep", "seq", None),
            P(),
            P(),
            P("rep", None),
        ),
        out_specs=(
            P("rep", "seq", None),
            P("rep", "seq", None),
            P("rep", "seq", None),
            P("rep", "seq", None),
            P("rep", None, "seq"),
            P(),
        ),
        check_vma=False,
    )
```

time: 1180 us -> 105 us (0.09); the launches traced: 1160 us -> 104 us
  waiting for transfers between devices: 868 us -> 0 us
  Pallas kernels: 0 us -> 98.1 us
  blocking collectives: 90.6 us -> 0 us
  local copies, waits for them, and re-layouts: 92.9 us -> 5.37 us
  other arithmetic: 34.9 us -> 0 us
  matrix products: 29.6 us -> 0 us
  loops' own time: 28.1 us -> 0 us
  between operations: 14 us -> 0.7 us
    unnamed x6 -> x0, waiting for transfers between devices: 714 us -> none
    pallas_call x0 -> x3, Pallas kernels: none -> 98.1 us  [the longest x1 63.5 us: scatter(): pl.pallas_call(scatter_kernel, out_shape=(rows, rows, jax.ShapeDtypeStruc...]
    reduce_scatter x2 -> x0, waiting for transfers between devices: 94.8 us -> none  [the longest x1 80.1 us: full_reduce(): lax.psum_scatter(key_rows_all.astype(jnp.bfloat16), 'seq', scatter_dimens...]
    psum x1 -> x0, blocking collectives: 64.8 us -> none  [on_device(): lax.psum(jnp.stack([query_gain_part, key_gain_part]), ('seq', 'rep'))]
    all_gather x2 -> x0, waiting for transfers between devices: 59.4 us -> none  [the longest x1 43.3 us: on_device(): lax.all_gather(key_normed, 'seq', axis=0, tiled=True)]
    dot_general x32 -> x0, matrix products: 29.6 us -> none  [the longest x8 15.3 us: contract_first(): lax.dot_general(left_rows, right_rows, (((0,), (0,)), ((), ())), preferre...]
    another operation x14 -> x0, loops' own time: 28.1 us -> none  [the longest x1 13.6 us: on_device(): lax.scan(task_step, zero_parts, (query_tiles, grad_tiles, out_tiles, own_...]
    dynamic_slice x40 -> x0, local copies, waits for them, and re-layouts: 27.9 us -> none  [the longest x12 9.39 us: block_scores(): key_gate = lax.dynamic_slice_in_dim(gate_pad, block_first, key_span, 1)]
  transfers between devices with their start and end apart: 5 -> 0, of which waited for: 5 -> 0; matrix products, arithmetic and copies ran while one was open for 2% -> 0% of each run, Pallas kernels for 0% -> 0%
where the time goes in v1:
time: 105 us; the launch traced here: 104 us
  Pallas kernels  98.1 us (93%)
  local copies, waits for them, and re-layouts  5.37 us (5%)
    pallas_call x1, Pallas kernels, scatter(): pl.pallas_call(scatter_kernel, out_shape=(rows, rows, jax.ShapeDtypeStruc...  63.5 us
    pallas_call x1, Pallas kernels, gather(): pl.pallas_call(gather_kernel, out_shape=jax.ShapeDtypeStruct((SHARDS, ROW...  26.6 us
    pallas_call x1, Pallas kernels, attend(): pl.pallas_call(attend_kernel, out_shape=(wide, wide, jax.ShapeDtypeStruct...  8.06 us
    unnamed x14, local copies, waits for them, and re-layouts  5.37 us

profile of v1, /device:TPU:0, one launch (start us, length us, event | category | flops | bytes accessed | tf_op | source)
XLA Modules:
  0.0 104.2 jit_solution(17720087241024830017)
XLA Ops:
  0.6 0.0 copy-start.1
  0.6 0.0 copy-start.2
  0.7 0.0 copy-start.3
  0.7 26.6 %gather_shards.1.kv_ref = bf16[32,272,256]{2,1,0:T(8,128)(2,1)} custom-call(bf16[256,128]{1,0:T(8,128)(2,1)} %bitcast.14, bf16[256,128]{1,0:T(8,128)(2,1)} %bitcast.26, bf16[4,256]{1,0:T(4,128)(2,1)} %bitcast.18, f32[1,128]{1,0:T(1,128)} %bitcast.20), custom_call_target="tpu_custom_call" | custom-call | tf_op jit(solution)/shard_map/gather_shards/pallas_call | solution.py:220
  27.2 8.1 %attend_both.1 = (bf16[256,512]{1,0:T(8,128)(2,1)}, bf16[256,512]{1,0:T(8,128)(2,1)}, bf16[32,272,256]{2,1,0:T(8,128)(2,1)}, f32[8,128]{1,0:T(8,128)}) custom-call(s32[1]{0:T(128)} %bitcast.place_ref, s32[4]{0:T(128)} %bitcast.27, bf16[32,272,256]{2,1,0:T(8,128)(2,1)} %gather_shards.1.kv_ref, bf16[256,512]{1,0:T(8,128)(2,1)} %bitcast.24, ...), custom_call_target="tpu_custom_call" | custom-call | tf_op jit(solution)/shard_map/attend_both/pallas_call | solution.py:428
  35.3 0.0 copy-done.1
  35.3 0.0 copy-done.2
  35.3 0.0 copy-done.3
  35.3 0.0 copy-start
  35.3 2.3 %copy-done = bf16[32,272,256]{2,1,0:T(8,128)(2,1)S(1)} copy-done((bf16[32,272,256]{2,1,0:T(8,128)(2,1)S(1)}, bf16[32,272,256]{2,1,0:T(8,128)(2,1)}, u32[]{:S(2)}) %copy-start) | copy-done | bytes 4456472
  37.6 0.0 copy-start.4
  37.6 0.7 copy-done.4
  38.3 63.5 %scatter_sums.1 = (bf16[256,128]{1,0:T(8,128)(2,1)S(1)}, bf16[256,128]{1,0:T(8,128)(2,1)S(1)}, f32[4,256]{1,0:T(4,128)S(1)}, f32[2,128]{1,0:T(2,128)S(1)}) custom-call(bf16[32,272,256]{2,1,0:T(8,128)(2,1)S(1)} %copy-done, f32[8,128]{1,0:T(8,128)S(1)} %copy-done.4, bf16[256,128]{1,0:T(8,128)(2,1)S(1)} %bitcast.15, bf16[4,256]{1,0:T(4,128)(2,1)S(1)} %bitcast.19, ...), custom_call_target="tpu_custom_call" | custom-call | tf_op jit(solution)/shard_map/scatter_sums/pallas_call | solution.py:660
  101.8 0.6 copy.18
  102.4 0.6 copy.19
  103.1 0.6 copy.20
  103.7 0.6 copy.21
Async XLA Ops:
  0.6 34.7 %copy-start.1 = (bf16[1,256,128]{2,1,0:T(8,128)(2,1)S(1)}, bf16[1,256,128]{2,1,0:T(8,128)(2,1)}, u32[]{:S(2)}) copy-start(bf16[1,256,128]{2,1,0:T(8,128)(2,1)} %param.9) | copy-start | bytes 196612
  0.6 34.7 %copy-start.2 = (bf16[1,4,256]{2,1,0:T(4,128)(2,1)S(1)}, bf16[1,4,256]{2,1,0:T(4,128)(2,1)}, u32[]{:S(2)}) copy-start(bf16[1,4,256]{2,1,0:T(4,128)(2,1)} %param.11) | copy-start | bytes 6148
  0.7 34.7 %copy-start.3 = (f32[128]{0:T(128)S(1)}, f32[128]{0:T(128)}, u32[]{:S(2)}) copy-start(f32[128]{0:T(128)} %param.14) | copy-start | bytes 1540
  35.3 2.3 %copy-start = (bf16[32,272,256]{2,1,0:T(8,128)(2,1)S(1)}, bf16[32,272,256]{2,1,0:T(8,128)(2,1)}, u32[]{:S(2)}) copy-start(bf16[32,272,256]{2,1,0:T(8,128)(2,1)} %get-tuple-element.16.part_ref) | copy-start | bytes 13369348
  37.6 0.7 copy-start.4

commit v2 on v1

v2 whole, which is shorter than its diff:
```python
import functools
import math

import jax
import jax.numpy as jnp
from jax import lax
from jax.experimental import pallas as pl
from jax.experimental.pallas import tpu as pltpu
from jax.sharding import PartitionSpec as P

MESH = pl.DeviceIdType.MESH
F32 = jnp.float32
BF16 = jnp.bfloat16

EPS = 1e-06
HEADS = 4
DH = 128
TOK = 256
TILE = 64
SHARDS = 32
HEAD_ROWS = 16
ROWS = HEAD_ROWS + TOK
PIECES = ((0, 80), (80, 144), (144, 208), (208, 272))
LOG2E = math.log2(math.e)
LN2 = math.log(2.0)
FAR = (2, -1, 1, 0)
BACK = 24
ORDER = (
    (0, 0), (-1, 0), (0, -1), (1, 0), (0, 1), (-1, -1), (-1, 1), (1, -1),
    (1, 1), (2, 0), (0, 2), (2, -1), (-1, 2), (2, 1), (1, 2), (2, 2),
)
STEPS = len(ORDER)


def spot():
    me = lax.axis_index("seq")
    return me // 8, (me // 2) % 4, me % 2


def shard_at(tree, da, db, core=None):
    z, y, c = spot()
    dz, dy = (da, db) if tree == 0 else (db, da)
    c = c if core is None else core
    return (((z + dz + 4) % 4) * 4 + (y + dy + 4) % 4) * 2 + c


def cell_at(tree, da, db):
    z, y, _ = spot()
    dz, dy = (da, db) if tree == 0 else (db, da)
    return ((z + dz + 4) % 4) * 4 + (y + dy + 4) % 4


def piece(tree, part):
    low, high = PIECES[2 * tree], PIECES[2 * tree + 1]
    first, last = {"a": low, "b": high, "ab": (low[0], high[1])}[part]
    return first, last - first


def rows_of(tree, part):
    first, count = piece(tree, part)
    return pl.ds(first, count)


def greet(devices):
    barrier = pltpu.get_barrier_semaphore()
    for device in devices:
        pl.semaphore_signal(barrier, inc=1, device_id=device, device_id_type=MESH)
    pl.semaphore_wait(barrier, len(devices))


def ring_events():
    names = ["A-", "A+", "A2a", "A2b"]
    for da in FAR:
        names += [("B-", da), ("B+", da), ("B2a", da), ("B2b", da)]
    return names


def split3(x):
    high = x.astype(BF16)
    rest = x - high.astype(F32)
    mid = rest.astype(BF16)
    low = (rest - mid.astype(F32)).astype(BF16)
    return high, mid, low


def row_to_columns(row):
    parts = [
        jnp.transpose(jnp.broadcast_to(row[:, half * DH : (half + 1) * DH], (DH, DH)))
        for half in (0, 1)
    ]
    return jnp.concatenate(parts, axis=0)


def split_lanes(full):
    high, mid, low = split3(full)
    lane = lax.broadcasted_iota(jnp.int32, full.shape, 1)
    picked = jnp.where(
        lane == 0,
        high.astype(F32),
        jnp.where(lane == 1, mid.astype(F32), jnp.where(lane == 2, low.astype(F32), 0.0)),
    )
    return picked.astype(BF16)


def contract_last(left, right):
    return lax.dot_general(left, right, (((1,), (1,)), ((), ())), preferred_element_type=F32)


def contract_first(left, right):
    return lax.dot_general(left, right, (((0,), (0,)), ((), ())), preferred_element_type=F32)


def pick(step, entries):
    found = jnp.int32(entries[0])
    for i, entry in enumerate(entries):
        if i:
            found = jnp.where(step == i, jnp.int32(entry), found)
    return found


def step_of(tree, da, db):
    return ORDER.index((da, db) if tree == 0 else (db, da))


def fused_kernel(
    length_ref,
    key_ref,
    value_ref,
    logit_ref,
    query_ref,
    grad_ref,
    query_gain_ref,
    key_gain_ref,
    att_ref,
    query_grad_ref,
    key_grad_ref,
    value_grad_ref,
    forget_grad_ref,
    gain_out_ref,
    shards,
    chunk_sum,
    base,
    query_wide,
    query_low,
    grad_wide,
    grad_low,
    prob,
    score_low,
    out_sum,
    key_gain_sum,
    offset,
    parts,
    twin,
    total,
    landed,
    small,
    small_landed,
    out_send,
    out_recv,
    back_send,
    back_recv,
    sum_send,
    sum_recv,
    small_send,
    small_recv,
):
    me = lax.axis_index("seq")
    z, y, core = spot()
    rep = lax.axis_index("rep")
    sibling = {"seq": shard_at(0, 0, 0, 1 - core)}
    partners = [[sibling]]
    partners.append([{"seq": shard_at(0, step, 0)} for step in (1, 2, 3)])
    partners.append([{"seq": shard_at(1, step, 0)} for step in (1, 2, 3)])
    partners.append([{"rep": (rep + step) % 4} for step in (1, 2, 3)])
    greet([device for group in partners for device in group])

    def remote(source, target, sends, receives, number, device):
        return pltpu.make_async_remote_copy(
            src_ref=source,
            dst_ref=target,
            send_sem=sends.at[number],
            recv_sem=receives.at[number],
            device_id=device,
            device_id_type=MESH,
        )


    raw = key_ref[...].astype(F32)
    scale = lax.rsqrt(jnp.mean(raw * raw, axis=1, keepdims=True) + EPS)
    shards[me, HEAD_ROWS:, 0:DH] = (raw * scale * key_gain_ref[...]).astype(BF16)
    shards[me, HEAD_ROWS:, DH:] = value_ref[...]
    logit = logit_ref[...].astype(F32)
    decay = jnp.minimum(logit, 0.0) - jnp.log1p(jnp.exp(-jnp.abs(logit)))
    row = lax.broadcasted_iota(jnp.int32, (TOK, TOK), 0)
    col = lax.broadcasted_iota(jnp.int32, (TOK, TOK), 1)
    upper = (row <= col).astype(F32)
    local = jnp.dot(decay, upper, preferred_element_type=F32, precision=lax.Precision.HIGHEST)
    local = local * LOG2E
    high = local.astype(BF16).astype(F32)
    mid = (local - high).astype(BF16).astype(F32)
    packed = [high, mid, local - high - mid, jnp.zeros((4, TOK), F32)]
    shards[me, 0:HEAD_ROWS, :] = jnp.concatenate(packed, axis=0).astype(BF16)

    ids = {}
    for tree in (0, 1):
        for name in ring_events():
            ids[tree, name] = len(ids)
    rings = len(ids)


    sent = []

    def send(event, tree, da, db, part, target):
        place = shards.at[shard_at(tree, da, db), rows_of(tree, part)]
        device = {"seq": shard_at(tree, *target)}
        remote(place, place, out_send, out_recv, ids[event], device).start()
        sent.append((ids[event], tree, part))

    def share(tree, da, db):
        place = shards.at[shard_at(tree, da, db), rows_of(tree, "ab")]
        number = rings + 2 * step_of(tree, da, db) + tree
        remote(place, place, out_send, out_recv, number, sibling).start()
        sent.append((number, tree, "ab"))

    def wait(tree, name, da, db, part):
        place = shards.at[shard_at(tree, da, db), rows_of(tree, part)]
        remote(place, place, out_send, out_recv, ids[tree, name], sibling).wait_recv()

    for tree in (0, 1):
        send((tree, "A-"), tree, 0, 0, "ab", (1, 0))
        send((tree, "A+"), tree, 0, 0, "ab", (-1, 0))

    chunk_sum[core, y, z] = jnp.concatenate(
        [jnp.broadcast_to(local[:, TOK - 1 :], (4, DH)), jnp.zeros((4, DH), F32)], axis=0
    )

    def sum_copies(axis):
        if axis == 0:
            place = chunk_sum.at[core, y, z]
        elif axis == 1:
            place = chunk_sum.at[core, y]
        else:
            place = chunk_sum.at[core]
        devices = partners[axis + 1] if axis < 2 else partners[0]
        return [
            remote(place, place, sum_send, sum_recv, 3 * axis + i, device)
            for i, device in enumerate(devices)
        ]

    def sum_wait(axis):
        for i in range(3 if axis < 2 else 1):
            if axis == 0:
                place = chunk_sum.at[core, y, (z + 3 - i) % 4]
            elif axis == 1:
                place = chunk_sum.at[core, (y + 3 - i) % 4]
            else:
                place = chunk_sum.at[1 - core]
            remote(place, place, sum_send, sum_recv, 3 * axis + i, sibling).wait_recv()

    for made in sum_copies(0):
        made.start()
    for tree in (0, 1):
        send((tree, ("B-", 0)), tree, 0, 0, "ab", (0, 1))
        send((tree, ("B+", 0)), tree, 0, 0, "ab", (0, -1))
        share(tree, 0, 0)

    def axis_near():
        for tree in (0, 1):
            wait(tree, "A-", -1, 0, "ab")
            send((tree, "A2a"), tree, -1, 0, "a", (1, 0))
            wait(tree, "A+", 1, 0, "ab")
            send((tree, "A2b"), tree, 1, 0, "b", (-1, 0))
            for da in (-1, 1):
                send((tree, ("B-", da)), tree, da, 0, "ab", (0, 1))
                send((tree, ("B+", da)), tree, da, 0, "ab", (0, -1))
                share(tree, da, 0)

    def axis_far():
        for tree in (0, 1):
            wait(tree, "A2a", 2, 0, "a")
            wait(tree, "A2b", 2, 0, "b")
            send((tree, ("B-", 2)), tree, 2, 0, "ab", (0, 1))
            send((tree, ("B+", 2)), tree, 2, 0, "ab", (0, -1))
            share(tree, 2, 0)

    def near(da):
        for tree in (0, 1):
            wait(tree, ("B-", da), da, -1, "ab")
            send((tree, ("B2a", da)), tree, da, -1, "a", (0, 1))
            wait(tree, ("B+", da), da, 1, "ab")
            send((tree, ("B2b", da)), tree, da, 1, "b", (0, -1))
            share(tree, da, -1)
            share(tree, da, 1)

    def far(da):
        for tree in (0, 1):
            wait(tree, ("B2a", da), da, 2, "a")
            wait(tree, ("B2b", da), da, 2, "b")
            share(tree, da, 2)

    gather_steps = {
        0: [axis_near],
        1: [functools.partial(near, 0)],
        2: [axis_far],
        3: [functools.partial(near, -1)],
        4: [functools.partial(near, 1)],
        5: [functools.partial(far, 0)],
        6: [functools.partial(near, 2)],
        7: [functools.partial(far, -1)],
        8: [functools.partial(far, 1)],
        9: [functools.partial(far, 2)],
    }


    ones = jnp.ones((TOK, DH), BF16)
    starts = []
    for tile in range(TOK // TILE):
        at = me * (TOK // TILE) + tile
        end = jnp.int32(0)
        start = jnp.int32(0)
        for document in range(4):
            end = end + length_ref[document]
            start = jnp.where(end <= at, end, start)
        starts.append(start * TILE)
    query_scale = query_gain_ref[...] * (DH**-0.5)
    for head in range(HEADS):
        raw = query_ref[:, head * DH : (head + 1) * DH].astype(F32)
        scale = lax.rsqrt(jnp.mean(raw * raw, axis=1, keepdims=True) + EPS)
        normed = (raw * scale * (query_scale * LOG2E)).astype(BF16)
        own_gate = row_to_columns(local[head : head + 1, :])
        query_low[head * TOK : (head + 1) * TOK, :] = normed
        query_wide[head] = jnp.concatenate([normed, split_lanes(own_gate)], axis=1)
    out_sum[...] = jnp.zeros_like(out_sum)
    key_gain_sum[...] = jnp.zeros_like(key_gain_sum)
    offset[...] = jnp.zeros_like(offset)
    lane_token = lax.broadcasted_iota(jnp.int32, (1, TOK), 1)

    def forward_block(block, diagonal):
        keys = shards[block, HEAD_ROWS:, 0:DH]
        values = shards[block, HEAD_ROWS:, DH:]
        key_wide = jnp.concatenate([keys, ones], axis=1)
        value_wide = jnp.concatenate([values, ones], axis=1)
        token = block * TOK + lane_token
        packed = shards[block, 0:HEAD_ROWS, :].astype(F32)
        gate = packed[0:4] + packed[4:8] + packed[8:12]
        if not diagonal:
            before = base[block, 0:4, :]
            gate = gate + jnp.concatenate([before, before], axis=1)
        for head in range(HEADS):
            scores = contract_last(query_wide[head], key_wide)
            pieces = []
            for tile in range(TOK // TILE):
                low = jnp.where(token >= starts[tile], gate[head : head + 1], jnp.inf)
                pieces.append(scores[tile * TILE : (tile + 1) * TILE] - low)
            scores = jnp.concatenate(pieces, axis=0)
            if diagonal:
                row = lax.broadcasted_iota(jnp.int32, (TOK, TOK), 0)
                col = lax.broadcasted_iota(jnp.int32, (TOK, TOK), 1)
                scores = jnp.where(col <= row, scores, -jnp.inf)
            weights = jnp.exp2(scores).astype(BF16)
            prob[me - block, head * TOK : (head + 1) * TOK, :] = weights
            out_sum[head] += jnp.dot(weights, value_wide, preferred_element_type=F32)

    sum_wait(0)
    for made in sum_copies(1):
        made.start()
    forward_block(me, True)
    sum_wait(1)
    for made in sum_copies(2):
        made.start()
    sum_wait(2)

    carry = jnp.zeros((8, DH), F32)
    for shard in range(SHARDS - 1, -1, -1):
        chunk = chunk_sum[shard % 2, (shard // 2) % 4, shard // 8]
        carry = carry - jnp.where(shard < me, chunk, 0.0)
        base[shard] = carry

    def chip_of(step):
        dz = pick(step, [entry[0] for entry in ORDER])
        dy = pick(step, [entry[1] for entry in ORDER])
        return cell_at(0, dz, dy)

    def forward_step(step, _):
        for at, actions in gather_steps.items():

            @pl.when(step == at)
            def _():
                for action in actions:
                    action()

        cell = chip_of(step)

        def one(which, _):
            block = cell * 2 + jnp.where(which == 0, core, 1 - core)

            @pl.when(which == 1)
            def _():
                for tree in (0, 1):
                    place = shards.at[block, rows_of(tree, "ab")]
                    number = rings + 2 * step + tree
                    remote(place, place, out_send, out_recv, number, sibling).wait_recv()

            @pl.when((block < me) & (block >= me - BACK))
            def _():
                forward_block(block, False)

            return 0

        return lax.fori_loop(0, 2, one, 0)

    lax.fori_loop(0, STEPS, forward_step, 0)

    for head in range(HEADS):
        span = slice(head * DH, (head + 1) * DH)
        inverse = 1.0 / out_sum[head, :, DH:]
        out = out_sum[head, :, 0:DH] * inverse
        att_ref[:, span] = out.astype(BF16)
        scaled = (grad_ref[:, span].astype(F32) * inverse).astype(BF16)
        inner = jnp.sum(scaled.astype(F32) * out, axis=1, keepdims=True)
        grad_low[head * TOK : (head + 1) * TOK, :] = scaled
        grad_wide[head] = jnp.concatenate(
            [scaled, split_lanes(jnp.broadcast_to(-inner, (TOK, DH)))], axis=1
        )
    out_sum[...] = jnp.zeros_like(out_sum)


    back = []

    def land(tree, name, part):
        first, count = piece(tree, part)
        return landed.at[ids[tree, name], pl.ds(first - piece(tree, "ab")[0], count)]

    def give(event, tree, da, db, part, target):
        source = total.at[cell_at(tree, da, db), rows_of(tree, part)]
        device = {"seq": shard_at(tree, *target)}
        goal = land(event[0], event[1], part)
        remote(source, goal, back_send, back_recv, ids[event], device).start()
        back.append((ids[event], event[0], event[1], part))

    def landing(tree, name, part):
        goal = land(tree, name, part)
        remote(goal, goal, back_send, back_recv, ids[tree, name], sibling).wait_recv()
        return goal[...]

    def added(terms):
        return functools.reduce(lambda a, b: a + b, [term.astype(F32) for term in terms])

    def put(tree, da, db, part, terms):
        whole = added(terms)
        if tree == 0 and part in ("a", "ab"):
            gates = whole[0:8] + whole[8:16]
            high = gates.astype(BF16).astype(F32)
            whole = jnp.concatenate([high, gates - high, whole[16:]], axis=0)
        total[cell_at(tree, da, db), rows_of(tree, part), :] = whole.astype(BF16)

    def twins(tree, da, db, part):
        place, rows = cell_at(tree, da, db), rows_of(tree, part)
        return [parts[shard_at(tree, da, db), rows, :], twin[place, rows, :]]

    def reduce_item(tree, da, db):
        if db == 2:
            put(tree, da, 2, "ab", twins(tree, da, 2, "ab"))
            give((tree, ("B2a", da)), tree, da, 2, "a", (0, 1))
            give((tree, ("B2b", da)), tree, da, 2, "b", (0, -1))
        elif db in (1, -1):
            name, close, away = ("B2a", "a", "b") if db == 1 else ("B2b", "b", "a")
            put(tree, da, db, away, twins(tree, da, db, away))
            put(tree, da, db, close, twins(tree, da, db, close) + [landing(tree, (name, da), close)])
            give((tree, ("B-" if db == 1 else "B+", da)), tree, da, db, "ab", (0, db))
        else:
            terms = twins(tree, da, 0, "ab")
            terms += [landing(tree, (name, da), "ab") for name in ("B-", "B+")]
            if da == 0:
                terms += [landing(tree, name, "ab") for name in ("A-", "A+")]
                return added(terms)
            put(tree, da, 0, "ab", terms)
            if da == 2:
                give((tree, "A2a"), tree, 2, 0, "a", (1, 0))
                give((tree, "A2b"), tree, 2, 0, "b", (-1, 0))
            else:
                name, part = ("A2a", "a") if da == 1 else ("A2b", "b")
                mine = total[cell_at(tree, da, 0), rows_of(tree, part), :]
                put(tree, da, 0, part, [mine, landing(tree, name, part)])
                give((tree, "A-" if da == 1 else "A+"), tree, da, 0, "ab", (da, 0))
        return None

    def twin_copy(step, source, cell):
        return remote(parts.at[source], twin.at[cell], back_send, back_recv, rings + step, sibling)

    def reduce_chip(at):
        dz, dy = ORDER[at]
        twin_copy(at, cell_at(0, dz, dy) * 2, cell_at(0, dz, dy)).wait_recv()
        return [reduce_item(0, dz, dy), reduce_item(1, dy, dz)]


    def backward_block(block):
        keys = shards[block, HEAD_ROWS:, 0:DH]
        values = shards[block, HEAD_ROWS:, DH:]
        key_wide = jnp.concatenate([keys, ones], axis=1)
        value_wide = jnp.concatenate([values, ones], axis=1)
        sums = []
        for head in range(HEADS):
            span = slice(head * TOK, (head + 1) * TOK)
            prob_grad = contract_last(grad_wide[head], value_wide)
            score_grad = prob[me - block, span, :].astype(F32) * prob_grad
            low = score_grad.astype(BF16)
            folded = jnp.sum(low.astype(F32).reshape(TOK // 8, 8, TOK), axis=0)
            sums.append(jnp.sum(folded, axis=0, keepdims=True))
            score_low[span, :] = low
            out_sum[head] += jnp.dot(low, key_wide, preferred_element_type=F32)
        key_part = contract_first(score_low[...], query_low[...]) * LN2
        value_part = contract_first(prob[me - block], grad_low[...])
        parts[block, HEAD_ROWS:, 0:DH] = key_part.astype(BF16)
        parts[block, HEAD_ROWS:, DH:] = value_part.astype(BF16)
        moved = (key_part * keys.astype(F32)).reshape(TOK // 8, 8, DH)
        key_gain_sum[...] += jnp.sum(moved, axis=0)
        columns = jnp.concatenate(sums + [jnp.zeros((4, TOK), F32)], axis=0)
        high = columns.astype(BF16).astype(F32)
        parts[block, 0:HEAD_ROWS, :] = jnp.concatenate([-high, high - columns], axis=0).astype(BF16)
        lane = lax.broadcasted_iota(jnp.int32, (8, DH), 1)
        whole = jnp.broadcast_to(jnp.sum(columns, axis=1, keepdims=True), (8, DH))
        offset[...] += jnp.where((lane >= block) & (lane < me), whole, 0.0)

    def backward_step(turn, _):
        step = STEPS - 1 - turn
        cell = chip_of(step)

        def one(which, _):
            block = cell * 2 + jnp.where(which == 1, core, 1 - core)
            used = (block <= me) & (block >= me - BACK)

            @pl.when(used)
            def _():
                backward_block(block)

            @pl.when(jnp.logical_not(used))
            def _():
                parts[block] = jnp.zeros((ROWS, 2 * DH), BF16)

            @pl.when(which == 0)
            def _():
                twin_copy(step, block, cell).start()

            return 0

        lax.fori_loop(0, 2, one, 0)
        for at in range(STEPS - 1, 0, -1):

            @pl.when(step == at - 1)
            def _():
                reduce_chip(at)

        return 0

    lax.fori_loop(0, STEPS, backward_step, 0)


    query_gain_sum = jnp.zeros((1, DH), F32)
    turned = []
    for head in range(HEADS):
        span = slice(head * DH, (head + 1) * DH)
        raw = query_ref[:, span].astype(F32)
        scale = lax.rsqrt(jnp.mean(raw * raw, axis=1, keepdims=True) + EPS)
        hat = raw * scale
        cotangent = out_sum[head, :, 0:DH]
        query_gain_sum += jnp.sum(cotangent * hat, axis=0, keepdims=True)
        inner = cotangent * query_scale
        mean = jnp.mean(inner * hat, axis=1, keepdims=True)
        query_grad_ref[:, span] = (scale * (inner - hat * mean)).astype(BF16)
        halves = [jnp.transpose(out_sum[head, half * DH : (half + 1) * DH, DH:])[0:1] for half in (0, 1)]
        turned.append(jnp.concatenate(halves, axis=1))
    row_sums = jnp.concatenate(turned, axis=0)
    query_gain_sum = query_gain_sum * (DH**-0.5)
    key_gain_row = jnp.sum(key_gain_sum[...], axis=0, keepdims=True) / key_gain_ref[...]
    small[0] = jnp.concatenate(
        [query_gain_sum, key_gain_row, jnp.zeros((6, DH), F32), offset[...]], axis=0
    )

    firsts = (0, 1, 4, 7)

    def small_copies(axis):
        return [
            remote(
                small.at[axis], small_landed.at[firsts[axis] + i], small_send, small_recv, firsts[axis] + i, device
            )
            for i, device in enumerate(partners[axis])
        ]

    def small_start(axis):
        for made in small_copies(axis):
            made.start()

    def small_add(axis):
        whole = small[axis]
        for i, made in enumerate(small_copies(axis)):
            made.wait_recv()
            whole = whole + small_landed[firsts[axis] + i]
        for made in small_copies(axis):
            made.wait_send()
        small[axis + 1] = whole

    small_start(0)
    finals = reduce_chip(0)
    small_add(0)
    small_start(1)

    whole = jnp.concatenate([finals[0][HEAD_ROWS:], finals[1]], axis=0)
    value_grad_ref[...] = whole[:, DH:].astype(BF16)
    cotangent = whole[:, 0:DH]
    raw = key_ref[...].astype(F32)
    scale = lax.rsqrt(jnp.mean(raw * raw, axis=1, keepdims=True) + EPS)
    hat = raw * scale
    inner = cotangent * key_gain_ref[...]
    mean = jnp.mean(inner * hat, axis=1, keepdims=True)
    key_grad_ref[...] = (scale * (inner - hat * mean)).astype(BF16)
    small_add(1)
    small_start(2)

    gates = finals[0][0:4] + finals[0][8:12] + row_sums
    row = lax.broadcasted_iota(jnp.int32, (TOK, TOK), 0)
    col = lax.broadcasted_iota(jnp.int32, (TOK, TOK), 1)
    lower = (row >= col).astype(F32)
    suffix = jnp.dot(gates, lower, preferred_element_type=F32, precision=lax.Precision.HIGHEST)
    logit = logit_ref[...].astype(F32)
    small_add(2)
    small_start(3)
    lane = lax.broadcasted_iota(jnp.int32, (4, DH), 1)
    later = jnp.sum(jnp.where(lane == me, small[3, 8:12, :], 0.0), axis=1, keepdims=True)
    forget_grad_ref[...] = (suffix + later) / (1.0 + jnp.exp(logit))
    small_add(3)
    gain_out_ref[...] = small[4, 0:2, :]

    for number, tree, part in sent:
        place = shards.at[0, rows_of(tree, part)]
        remote(place, place, out_send, out_recv, number, sibling).wait_send()
    for number, tree, name, part in back:
        goal = land(tree, name, part)
        remote(goal, goal, back_send, back_recv, number, sibling).wait_send()
    for at in range(STEPS):
        twin_copy(at, 0, 0).wait_send()
    for axis in range(3):
        for made in sum_copies(axis):
            made.wait_send()


def fused(lengths_row, key_local, value_local, logit_local, query_local, grad_local, query_gain, key_gain):
    vmem = pl.BlockSpec(memory_space=pltpu.VMEM)
    smem = pl.BlockSpec(memory_space=pltpu.SMEM)
    wide = jax.ShapeDtypeStruct((TOK, HEADS * DH), BF16)
    narrow = jax.ShapeDtypeStruct((TOK, DH), BF16)
    rows = HEADS * TOK
    dma = pltpu.SemaphoreType.DMA
    return pl.pallas_call(
        fused_kernel,
        out_shape=(
            wide,
            wide,
            narrow,
            narrow,
            jax.ShapeDtypeStruct((HEADS, TOK), F32),
            jax.ShapeDtypeStruct((2, DH), F32),
        ),
        in_specs=[smem] + [vmem] * 7,
        out_specs=(vmem,) * 6,
        scratch_shapes=[
            pltpu.VMEM((SHARDS, ROWS, 2 * DH), BF16),
            pltpu.VMEM((2, 4, 4, 8, DH), F32),
            pltpu.VMEM((SHARDS, 8, DH), F32),
            pltpu.VMEM((HEADS, TOK, 2 * DH), BF16),
            pltpu.VMEM((rows, DH), BF16),
            pltpu.VMEM((HEADS, TOK, 2 * DH), BF16),
            pltpu.VMEM((rows, DH), BF16),
            pltpu.VMEM((BACK + 1, rows, TOK), BF16),
            pltpu.VMEM((rows, TOK), BF16),
            pltpu.VMEM((HEADS, TOK, 2 * DH), F32),
            pltpu.VMEM((8, DH), F32),
            pltpu.VMEM((8, DH), F32),
            pltpu.VMEM((SHARDS, ROWS, 2 * DH), BF16),
            pltpu.VMEM((SHARDS // 2, ROWS, 2 * DH), BF16),
            pltpu.VMEM((SHARDS // 2, ROWS, 2 * DH), BF16),
            pltpu.VMEM((40, PIECES[1][1], 2 * DH), BF16),
            pltpu.VMEM((5, 16, DH), F32),
            pltpu.VMEM((10, 16, DH), F32),
            dma((40 + 2 * STEPS,)),
            dma((40 + 2 * STEPS,)),
            dma((40 + STEPS,)),
            dma((40 + STEPS,)),
            dma((7,)),
            dma((7,)),
            dma((10,)),
            dma((10,)),
        ],
        compiler_params=pltpu.CompilerParams(
            collective_id=0, has_side_effects=True, vmem_limit_bytes=56 * 2**20
        ),
        name="attend_whole",
    )(lengths_row, key_local, value_local, logit_local, query_local, grad_local, query_gain, key_gain)


def on_device(queries, key_vectors, values, forget_logit, out_grad, query_gain, key_gain, lengths):
    attention, query_grad, key_grad, value_grad, forget_grad, gain_grad = fused(
        lengths[0],
        key_vectors[0],
        values[0],
        forget_logit[0],
        queries[0],
        out_grad[0],
        query_gain.reshape(1, DH),
        key_gain.reshape(1, DH),
    )
    return (
        attention[None],
        query_grad[None],
        key_grad[None],
        value_grad[None],
        forget_grad[None],
        gain_grad,
    )


def solution(mesh):
    return jax.shard_map(
        on_device,
        mesh=mesh,
        in_specs=(
            P("rep", "seq", None),
            P("rep", "seq", None),
            P("rep", "seq", None),
            P("rep", None, "seq"),
            P("rep", "seq", None),
            P(),
            P(),
            P("rep", None),
        ),
        out_specs=(
            P("rep", "seq", None),
            P("rep", "seq", None),
            P("rep", "seq", None),
            P("rep", "seq", None),
            P("rep", None, "seq"),
            P(),
        ),
        check_vma=False,
    )
```

time: 105 us -> 99.5 us (0.948)
  Pallas kernels: 98.1 us -> 93.2 us
    pallas_call x3 -> x1, Pallas kernels: 98.1 us -> 93.2 us  [fused(): pl.pallas_call(fused_kernel, out_shape=(wide, wide, narrow, narrow, jax.S...]
    unnamed x14 -> x16, local copies, waits for them, and re-layouts: 5.37 us -> 5.34 us
where the time goes in v2:
time: 99.5 us; the launch traced here: 99.2 us
  Pallas kernels  93.2 us (94%)
  local copies, waits for them, and re-layouts  5.34 us (5%)
    pallas_call x1, Pallas kernels, fused(): pl.pallas_call(fused_kernel, out_shape=(wide, wide, narrow, narrow, jax.S...  93.2 us
    unnamed x16, local copies, waits for them, and re-layouts  5.34 us

profile of v2, /device:TPU:0, one launch (start us, length us, event | category | flops | bytes accessed | tf_op | source)
XLA Modules:
  0.0 99.2 jit_solution(8493571632567941936)
XLA Ops:
  0.6 93.2 %attend_whole.1 = (bf16[256,512]{1,0:T(8,128)(2,1)}, bf16[256,512]{1,0:T(8,128)(2,1)}, bf16[256,128]{1,0:T(8,128)(2,1)}, bf16[256,128]{1,0:T(8,128)(2,1)}, f32[4,256]{1,0:T(4,128)}, /*index=5*/f32[2,128]{1,0:T(2,128)}) custom-call(s32[4]{0:T(128)} %bitcast.23, bf16[256,128]{1,0:T(8,128)(2,1)} %bitcast.17, bf16[256,128]{1,0:T(8,128)(2,1)} %bitcast.18, ...), custom_call_target="tpu_custom_call" | custom-call | tf_op jit(solution)/shard_map/attend_whole/pallas_call | solution.py:654
  93.8 0.0 copy-start
  93.8 1.7 %copy.20 = bf16[1,256,512]{2,1,0:T(8,128)(2,1)} copy(bf16[1,256,512]{2,1,0:T(8,128)(2,1)} %bitcast.16) | data formatting | bytes 524288
  95.6 0.0 copy-done
  95.6 0.0 copy-start.2
  95.6 0.7 copy.21
  96.3 0.2 copy-done.2
  96.4 0.0 copy-start.1
  96.4 0.6 copy.22
  97.1 0.2 copy-done.1
  97.3 0.0 copy-start.3
  97.3 0.6 copy.23
  97.9 0.0 copy-done.3
  97.9 0.0 copy-start.4
  97.9 0.6 copy.24
  98.5 0.1 copy-done.4
  98.6 0.6 copy.25
Async XLA Ops:
  93.8 1.7 %copy-start = (bf16[256,512]{1,0:T(8,128)(2,1)S(1)}, bf16[256,512]{1,0:T(8,128)(2,1)}, u32[]{:S(2)}) copy-start(bf16[256,512]{1,0:T(8,128)(2,1)} %get-tuple-element.13) | copy-start | bytes 786436
  95.6 0.9 copy-start.2
  96.4 0.9 copy-start.1
  97.3 0.7 copy-start.3
  97.9 0.7 copy-start.4

commit v3 on v2

--- a/solution.py
+++ b/solution.py
@@ -30,24 +30,9 @@
     (1, 1), (2, 0), (0, 2), (2, -1), (-1, 2), (2, 1), (1, 2), (2, 2),
 )
 STEPS = len(ORDER)
-
-
-def spot():
-    me = lax.axis_index("seq")
-    return me // 8, (me // 2) % 4, me % 2
-
-
-def shard_at(tree, da, db, core=None):
-    z, y, c = spot()
-    dz, dy = (da, db) if tree == 0 else (db, da)
-    c = c if core is None else core
-    return (((z + dz + 4) % 4) * 4 + (y + dy + 4) % 4) * 2 + c
-
-
-def cell_at(tree, da, db):
-    z, y, _ = spot()
-    dz, dy = (da, db) if tree == 0 else (db, da)
-    return ((z + dz + 4) % 4) * 4 + (y + dy + 4) % 4
+LATE = (
+    (4, (1, 2, 1)), (4, (0, 2, 1)), (5, (1, 2, -1)), (6, (0, 2, -1)), (9, (1, 2, 0)), (9, (0, 2, 0)),
+)
 
 
 def piece(tree, part):
@@ -89,6 +74,12 @@
         for half in (0, 1)
     ]
     return jnp.concatenate(parts, axis=0)
+
+
+def turn(x):
+    if x.shape[0] == DH:
+        return jnp.concatenate([jnp.transpose(x[:, :DH]), jnp.transpose(x[:, DH:])], axis=0)
+    return jnp.concatenate([jnp.transpose(x[:DH]), jnp.transpose(x[DH:])], axis=1)
 
 
 def split_lanes(full):
@@ -106,15 +97,11 @@
     return lax.dot_general(left, right, (((1,), (1,)), ((), ())), preferred_element_type=F32)
 
 
-def contract_first(left, right):
-    return lax.dot_general(left, right, (((0,), (0,)), ((), ())), preferred_element_type=F32)
-
-
 def pick(step, entries):
-    found = jnp.int32(entries[0])
+    found = entries[0]
     for i, entry in enumerate(entries):
         if i:
-            found = jnp.where(step == i, jnp.int32(entry), found)
+            found = jnp.where(step == i, entry, found)
     return found
 
 
@@ -141,9 +128,9 @@
     chunk_sum,
     base,
     query_wide,
-    query_low,
+    query_turned,
     grad_wide,
-    grad_low,
+    grad_turned,
     prob,
     score_low,
     out_sum,
@@ -164,14 +151,31 @@
     small_send,
     small_recv,
 ):
-    me = lax.axis_index("seq")
-    z, y, core = spot()
-    rep = lax.axis_index("rep")
-    sibling = {"seq": shard_at(0, 0, 0, 1 - core)}
-    partners = [[sibling]]
-    partners.append([{"seq": shard_at(0, step, 0)} for step in (1, 2, 3)])
-    partners.append([{"seq": shard_at(1, step, 0)} for step in (1, 2, 3)])
-    partners.append([{"rep": (rep + step) % 4} for step in (1, 2, 3)])
+    me, rep = lax.axis_index("seq"), lax.axis_index("rep")
+    z, y, core = me // 8, (me // 2) % 4, me % 2
+    zs, ys, reps = (
+        {step: at if step == 0 else (at + (step + 4) % 4) % 4 for step in range(-3, 4)} for at in (z, y, rep)
+    )
+    cells = {(dz, dy): zs[dz] * 4 + ys[dy] for dz in FAR for dy in FAR}
+    places = {key: cell * 2 + core for key, cell in cells.items()}
+    other = 1 - core
+
+    def cell_at(tree, da, db):
+        return cells[(da, db) if tree == 0 else (db, da)]
+
+    def shard_at(tree, da, db):
+        return places[(da, db) if tree == 0 else (db, da)]
+
+    def device_at(tree, da, db):
+        return (shard_at(tree, da, db), rep)
+
+    sibling = (z * 8 + y * 2 + other, rep)
+    line_steps = [(dz, dc) for dz in range(4) for dc in range(2) if dz or dc]
+    field_steps = [(dy, dx) for dy in range(4) for dx in range(4) if dy or dx]
+    partners = [
+        [(zs[dz] * 8 + y * 2 + (other if dc else core), rep) for dz, dc in line_steps],
+        [(z * 8 + ys[dy] * 2 + core, reps[dx]) for dy, dx in field_steps],
+    ]
     greet([device for group in partners for device in group])
 
     def remote(source, target, sends, receives, number, device):
@@ -212,7 +216,7 @@
 
     def send(event, tree, da, db, part, target):
         place = shards.at[shard_at(tree, da, db), rows_of(tree, part)]
-        device = {"seq": shard_at(tree, *target)}
+        device = device_at(tree, *target)
         remote(place, place, out_send, out_recv, ids[event], device).start()
         sent.append((ids[event], tree, part))
 
@@ -230,32 +234,30 @@
         send((tree, "A-"), tree, 0, 0, "ab", (1, 0))
         send((tree, "A+"), tree, 0, 0, "ab", (-1, 0))
 
-    chunk_sum[core, y, z] = jnp.concatenate(
+    line = z * 2 + core
+    chunk_sum[y, line] = jnp.concatenate(
         [jnp.broadcast_to(local[:, TOK - 1 :], (4, DH)), jnp.zeros((4, DH), F32)], axis=0
     )
 
     def sum_copies(axis):
         if axis == 0:
-            place = chunk_sum.at[core, y, z]
-        elif axis == 1:
-            place = chunk_sum.at[core, y]
+            place, devices = chunk_sum.at[y, line], partners[0]
         else:
-            place = chunk_sum.at[core]
-        devices = partners[axis + 1] if axis < 2 else partners[0]
+            place = chunk_sum.at[y]
+            devices = [(z * 8 + ys[step] * 2 + core, rep) for step in (1, 2, 3)]
         return [
-            remote(place, place, sum_send, sum_recv, 3 * axis + i, device)
+            remote(place, place, sum_send, sum_recv, 7 * axis + i, device)
             for i, device in enumerate(devices)
         ]
 
     def sum_wait(axis):
-        for i in range(3 if axis < 2 else 1):
+        for i in range(3 if axis else 7):
             if axis == 0:
-                place = chunk_sum.at[core, y, (z + 3 - i) % 4]
-            elif axis == 1:
-                place = chunk_sum.at[core, (y + 3 - i) % 4]
+                dz, dc = line_steps[i]
+                place = chunk_sum.at[y, zs[-dz] * 2 + (other if dc else core)]
             else:
-                place = chunk_sum.at[1 - core]
-            remote(place, place, sum_send, sum_recv, 3 * axis + i, sibling).wait_recv()
+                place = chunk_sum.at[ys[-i - 1]]
+            remote(place, place, sum_send, sum_recv, 7 * axis + i, sibling).wait_recv()
 
     for made in sum_copies(0):
         made.start()
@@ -299,16 +301,14 @@
             share(tree, da, 2)
 
     gather_steps = {
-        0: [axis_near],
-        1: [functools.partial(near, 0)],
-        2: [axis_far],
-        3: [functools.partial(near, -1)],
-        4: [functools.partial(near, 1)],
-        5: [functools.partial(far, 0)],
-        6: [functools.partial(near, 2)],
-        7: [functools.partial(far, -1)],
-        8: [functools.partial(far, 1)],
-        9: [functools.partial(far, 2)],
+        0: axis_far,
+        1: functools.partial(near, -1),
+        2: functools.partial(near, 1),
+        3: functools.partial(far, 0),
+        4: functools.partial(near, 2),
+        5: functools.partial(far, -1),
+        6: functools.partial(far, 1),
+        7: functools.partial(far, 2),
     }
 
 
@@ -328,7 +328,7 @@
         scale = lax.rsqrt(jnp.mean(raw * raw, axis=1, keepdims=True) + EPS)
         normed = (raw * scale * (query_scale * LOG2E)).astype(BF16)
         own_gate = row_to_columns(local[head : head + 1, :])
-        query_low[head * TOK : (head + 1) * TOK, :] = normed
+        query_turned[:, head * TOK : (head + 1) * TOK] = turn(normed.astype(F32)).astype(BF16)
         query_wide[head] = jnp.concatenate([normed, split_lanes(own_gate)], axis=1)
     out_sum[...] = jnp.zeros_like(out_sum)
     key_gain_sum[...] = jnp.zeros_like(key_gain_sum)
@@ -346,8 +346,11 @@
         if not diagonal:
             before = base[block, 0:4, :]
             gate = gate + jnp.concatenate([before, before], axis=1)
+        following = contract_last(query_wide[0], key_wide)
         for head in range(HEADS):
-            scores = contract_last(query_wide[head], key_wide)
+            scores = following
+            if head + 1 < HEADS:
+                following = contract_last(query_wide[head + 1], key_wide)
             pieces = []
             for tile in range(TOK // TILE):
                 low = jnp.where(token >= starts[tile], gate[head : head + 1], jnp.inf)
@@ -361,35 +364,28 @@
             prob[me - block, head * TOK : (head + 1) * TOK, :] = weights
             out_sum[head] += jnp.dot(weights, value_wide, preferred_element_type=F32)
 
+    forward_block(me, True)
     sum_wait(0)
     for made in sum_copies(1):
         made.start()
-    forward_block(me, True)
+    axis_near()
+    near(0)
     sum_wait(1)
-    for made in sum_copies(2):
-        made.start()
-    sum_wait(2)
 
     carry = jnp.zeros((8, DH), F32)
     for shard in range(SHARDS - 1, -1, -1):
-        chunk = chunk_sum[shard % 2, (shard // 2) % 4, shard // 8]
+        chunk = chunk_sum[(shard // 2) % 4, (shard // 8) * 2 + shard % 2]
         carry = carry - jnp.where(shard < me, chunk, 0.0)
         base[shard] = carry
 
     def chip_of(step):
-        dz = pick(step, [entry[0] for entry in ORDER])
-        dy = pick(step, [entry[1] for entry in ORDER])
-        return cell_at(0, dz, dy)
+        return pick(step, [cells[entry] for entry in ORDER])
 
     def forward_step(step, _):
-        for at, actions in gather_steps.items():
-
-            @pl.when(step == at)
-            def _():
-                for action in actions:
-                    action()
-
         cell = chip_of(step)
+
+        for at, action in gather_steps.items():
+            pl.when(step == at)(action)
 
         def one(which, _):
             block = cell * 2 + jnp.where(which == 0, core, 1 - core)
@@ -418,7 +414,7 @@
         att_ref[:, span] = out.astype(BF16)
         scaled = (grad_ref[:, span].astype(F32) * inverse).astype(BF16)
         inner = jnp.sum(scaled.astype(F32) * out, axis=1, keepdims=True)
-        grad_low[head * TOK : (head + 1) * TOK, :] = scaled
+        grad_turned[:, head * TOK : (head + 1) * TOK] = turn(scaled.astype(F32)).astype(BF16)
         grad_wide[head] = jnp.concatenate(
             [scaled, split_lanes(jnp.broadcast_to(-inner, (TOK, DH)))], axis=1
         )
@@ -433,7 +429,7 @@
 
     def give(event, tree, da, db, part, target):
         source = total.at[cell_at(tree, da, db), rows_of(tree, part)]
-        device = {"seq": shard_at(tree, *target)}
+        device = device_at(tree, *target)
         goal = land(event[0], event[1], part)
         remote(source, goal, back_send, back_recv, ids[event], device).start()
         back.append((ids[event], event[0], event[1], part))
@@ -488,10 +484,14 @@
     def twin_copy(step, source, cell):
         return remote(parts.at[source], twin.at[cell], back_send, back_recv, rings + step, sibling)
 
-    def reduce_chip(at):
+    def reduce_turn(turn):
+        at = STEPS - turn
         dz, dy = ORDER[at]
         twin_copy(at, cell_at(0, dz, dy) * 2, cell_at(0, dz, dy)).wait_recv()
-        return [reduce_item(0, dz, dy), reduce_item(1, dy, dz)]
+        items = [(0, dz, dy), (1, dy, dz)]
+        now = [item for item in items if item not in [late for _, late in LATE]]
+        now += [late for when, late in LATE if when == turn]
+        return [reduce_item(*item) for item in now]
 
 
     def backward_block(block):
@@ -500,21 +500,23 @@
         key_wide = jnp.concatenate([keys, ones], axis=1)
         value_wide = jnp.concatenate([values, ones], axis=1)
         sums = []
+        following = contract_last(grad_wide[0], value_wide)
         for head in range(HEADS):
             span = slice(head * TOK, (head + 1) * TOK)
-            prob_grad = contract_last(grad_wide[head], value_wide)
+            prob_grad = following
+            if head + 1 < HEADS:
+                following = contract_last(grad_wide[head + 1], value_wide)
             score_grad = prob[me - block, span, :].astype(F32) * prob_grad
             low = score_grad.astype(BF16)
             folded = jnp.sum(low.astype(F32).reshape(TOK // 8, 8, TOK), axis=0)
             sums.append(jnp.sum(folded, axis=0, keepdims=True))
             score_low[span, :] = low
             out_sum[head] += jnp.dot(low, key_wide, preferred_element_type=F32)
-        key_part = contract_first(score_low[...], query_low[...]) * LN2
-        value_part = contract_first(prob[me - block], grad_low[...])
-        parts[block, HEAD_ROWS:, 0:DH] = key_part.astype(BF16)
-        parts[block, HEAD_ROWS:, DH:] = value_part.astype(BF16)
-        moved = (key_part * keys.astype(F32)).reshape(TOK // 8, 8, DH)
-        key_gain_sum[...] += jnp.sum(moved, axis=0)
+        key_part = (jnp.dot(query_turned[...], score_low[...], preferred_element_type=F32) * LN2).astype(BF16)
+        value_part = jnp.dot(grad_turned[...], prob[me - block], preferred_element_type=F32)
+        parts[block, HEAD_ROWS : HEAD_ROWS + DH, :] = key_part
+        parts[block, HEAD_ROWS + DH :, :] = value_part.astype(BF16)
+        key_gain_sum[...] += jnp.dot(key_part, keys, preferred_element_type=F32)
         columns = jnp.concatenate(sums + [jnp.zeros((4, TOK), F32)], axis=0)
         high = columns.astype(BF16).astype(F32)
         parts[block, 0:HEAD_ROWS, :] = jnp.concatenate([-high, high - columns], axis=0).astype(BF16)
@@ -545,11 +547,11 @@
             return 0
 
         lax.fori_loop(0, 2, one, 0)
-        for at in range(STEPS - 1, 0, -1):
-
-            @pl.when(step == at - 1)
+        for at in range(1, STEPS):
+
+            @pl.when(turn == at)
             def _():
-                reduce_chip(at)
+                reduce_turn(at)
 
         return 0
 
@@ -572,50 +574,46 @@
         turned.append(jnp.concatenate(halves, axis=1))
     row_sums = jnp.concatenate(turned, axis=0)
     query_gain_sum = query_gain_sum * (DH**-0.5)
-    key_gain_row = jnp.sum(key_gain_sum[...], axis=0, keepdims=True) / key_gain_ref[...]
+    row = lax.broadcasted_iota(jnp.int32, (DH, DH), 0)
+    col = lax.broadcasted_iota(jnp.int32, (DH, DH), 1)
+    diagonal = jnp.where(row == col, key_gain_sum[...], 0.0)
+    key_gain_row = jnp.sum(diagonal, axis=0, keepdims=True) / key_gain_ref[...]
     small[0] = jnp.concatenate(
         [query_gain_sum, key_gain_row, jnp.zeros((6, DH), F32), offset[...]], axis=0
     )
 
-    firsts = (0, 1, 4, 7)
-
     def small_copies(axis):
         return [
-            remote(
-                small.at[axis], small_landed.at[firsts[axis] + i], small_send, small_recv, firsts[axis] + i, device
-            )
+            remote(small.at[axis], small_landed.at[7 * axis + i], small_send, small_recv, 7 * axis + i, device)
             for i, device in enumerate(partners[axis])
         ]
 
-    def small_start(axis):
-        for made in small_copies(axis):
-            made.start()
-
     def small_add(axis):
         whole = small[axis]
+        shared = lax.broadcasted_iota(jnp.int32, (16, DH), 0) < 8
         for i, made in enumerate(small_copies(axis)):
             made.wait_recv()
-            whole = whole + small_landed[firsts[axis] + i]
-        for made in small_copies(axis):
-            made.wait_send()
+            term = small_landed[7 * axis + i]
+            if axis == 1 and field_steps[i][1]:
+                term = jnp.where(shared, term, 0.0)
+            whole = whole + term
         small[axis + 1] = whole
 
-    small_start(0)
-    finals = reduce_chip(0)
+    for made in small_copies(0):
+        made.start()
+    finals = reduce_turn(STEPS)
     small_add(0)
-    small_start(1)
-
-    whole = jnp.concatenate([finals[0][HEAD_ROWS:], finals[1]], axis=0)
-    value_grad_ref[...] = whole[:, DH:].astype(BF16)
-    cotangent = whole[:, 0:DH]
+    for made in small_copies(1):
+        made.start()
+
+    value_grad_ref[...] = turn(finals[1]).astype(BF16)
+    cotangent = turn(finals[0][HEAD_ROWS:])
     raw = key_ref[...].astype(F32)
     scale = lax.rsqrt(jnp.mean(raw * raw, axis=1, keepdims=True) + EPS)
     hat = raw * scale
     inner = cotangent * key_gain_ref[...]
     mean = jnp.mean(inner * hat, axis=1, keepdims=True)
     key_grad_ref[...] = (scale * (inner - hat * mean)).astype(BF16)
-    small_add(1)
-    small_start(2)
 
     gates = finals[0][0:4] + finals[0][8:12] + row_sums
     row = lax.broadcasted_iota(jnp.int32, (TOK, TOK), 0)
@@ -623,13 +621,11 @@
     lower = (row >= col).astype(F32)
     suffix = jnp.dot(gates, lower, preferred_element_type=F32, precision=lax.Precision.HIGHEST)
     logit = logit_ref[...].astype(F32)
-    small_add(2)
-    small_start(3)
+    small_add(1)
     lane = lax.broadcasted_iota(jnp.int32, (4, DH), 1)
-    later = jnp.sum(jnp.where(lane == me, small[3, 8:12, :], 0.0), axis=1, keepdims=True)
+    later = jnp.sum(jnp.where(lane == me, small[2, 8:12, :], 0.0), axis=1, keepdims=True)
     forget_grad_ref[...] = (suffix + later) / (1.0 + jnp.exp(logit))
-    small_add(3)
-    gain_out_ref[...] = small[4, 0:2, :]
+    gain_out_ref[...] = small[2, 0:2, :]
 
     for number, tree, part in sent:
         place = shards.at[0, rows_of(tree, part)]
@@ -639,8 +635,8 @@
         remote(goal, goal, back_send, back_recv, number, sibling).wait_send()
     for at in range(STEPS):
         twin_copy(at, 0, 0).wait_send()
-    for axis in range(3):
-        for made in sum_copies(axis):
+    for axis in range(2):
+        for made in sum_copies(axis) + small_copies(axis):
             made.wait_send()
 
 
@@ -665,31 +661,31 @@
         out_specs=(vmem,) * 6,
         scratch_shapes=[
             pltpu.VMEM((SHARDS, ROWS, 2 * DH), BF16),
-            pltpu.VMEM((2, 4, 4, 8, DH), F32),
+            pltpu.VMEM((4, 8, 8, DH), F32),
             pltpu.VMEM((SHARDS, 8, DH), F32),
             pltpu.VMEM((HEADS, TOK, 2 * DH), BF16),
-            pltpu.VMEM((rows, DH), BF16),
+            pltpu.VMEM((DH, rows), BF16),
             pltpu.VMEM((HEADS, TOK, 2 * DH), BF16),
-            pltpu.VMEM((rows, DH), BF16),
+            pltpu.VMEM((DH, rows), BF16),
             pltpu.VMEM((BACK + 1, rows, TOK), BF16),
             pltpu.VMEM((rows, TOK), BF16),
             pltpu.VMEM((HEADS, TOK, 2 * DH), F32),
-            pltpu.VMEM((8, DH), F32),
+            pltpu.VMEM((DH, DH), F32),
             pltpu.VMEM((8, DH), F32),
             pltpu.VMEM((SHARDS, ROWS, 2 * DH), BF16),
             pltpu.VMEM((SHARDS // 2, ROWS, 2 * DH), BF16),
             pltpu.VMEM((SHARDS // 2, ROWS, 2 * DH), BF16),
             pltpu.VMEM((40, PIECES[1][1], 2 * DH), BF16),
-            pltpu.VMEM((5, 16, DH), F32),
-            pltpu.VMEM((10, 16, DH), F32),
+            pltpu.VMEM((3, 16, DH), F32),
+            pltpu.VMEM((22, 16, DH), F32),
             dma((40 + 2 * STEPS,)),
             dma((40 + 2 * STEPS,)),
             dma((40 + STEPS,)),
             dma((40 + STEPS,)),
-            dma((7,)),
-            dma((7,)),
             dma((10,)),
             dma((10,)),
+            dma((22,)),
+            dma((22,)),
         ],
         compiler_params=pltpu.CompilerParams(
             collective_id=0, has_side_effects=True, vmem_limit_bytes=56 * 2**20
@@ -698,8 +694,25 @@
     )(lengths_row, key_local, value_local, logit_local, query_local, grad_local, query_gain, key_gain)
 
 
+def write_kernel(*refs):
+    count = len(refs) // 2
+    for i in range(count):
+        refs[count + i][...] = refs[i][...]
+
+
+def write(*arrays):
+    vmem = pl.BlockSpec(memory_space=pltpu.VMEM)
+    return pl.pallas_call(
+        write_kernel,
+        out_shape=tuple(jax.ShapeDtypeStruct(a.shape, a.dtype) for a in arrays),
+        in_specs=[vmem] * len(arrays),
+        out_specs=(vmem,) * len(arrays),
+        name="write_results",
+    )(*arrays)
+
+
 def on_device(queries, key_vectors, values, forget_logit, out_grad, query_gain, key_gain, lengths):
-    attention, query_grad, key_grad, value_grad, forget_grad, gain_grad = fused(
+    results = fused(
         lengths[0],
         key_vectors[0],
         values[0],
@@ -709,6 +722,7 @@
         query_gain.reshape(1, DH),
         key_gain.reshape(1, DH),
     )
+    attention, query_grad, key_grad, value_grad, forget_grad, gain_grad = write(*results)
     return (
         attention[None],
         query_grad[None],

time: 99.5 us -> 83.4 us (0.84)
  Pallas kernels: 93.2 us -> 82.2 us
  local copies, waits for them, and re-layouts: 5.34 us -> 0 us
    pallas_call x1, Pallas kernels: 93.2 us -> 80.3 us  [fused(): pl.pallas_call(fused_kernel, out_shape=(wide, wide, narrow, narrow, jax.S...]
    unnamed x16 -> x0, local copies, waits for them, and re-layouts: 5.34 us -> none
    pallas_call x0 -> x1, Pallas kernels: none -> 1.92 us  [write(): pl.pallas_call(write_kernel, out_shape=tuple((jax.ShapeDtypeStruct(a.shap...]
where the time goes in v3:
time: 83.4 us; the launch traced here: 82.9 us
  Pallas kernels  82.2 us (99%)
    pallas_call x1, Pallas kernels, fused(): pl.pallas_call(fused_kernel, out_shape=(wide, wide, narrow, narrow, jax.S...  80.3 us
    pallas_call x1, Pallas kernels, write(): pl.pallas_call(write_kernel, out_shape=tuple((jax.ShapeDtypeStruct(a.shap...  1.92 us

profile of v3, /device:TPU:0, one launch (start us, length us, event | category | flops | bytes accessed | tf_op | source)
XLA Modules:
  0.0 82.9 jit_solution(5330313124770323581)
XLA Ops:
  0.6 80.3 %attend_whole.1 = (bf16[256,512]{1,0:T(8,128)(2,1)}, bf16[256,512]{1,0:T(8,128)(2,1)}, bf16[256,128]{1,0:T(8,128)(2,1)}, bf16[256,128]{1,0:T(8,128)(2,1)}, f32[4,256]{1,0:T(4,128)}, /*index=5*/f32[2,128]{1,0:T(2,128)}) custom-call(s32[4]{0:T(128)} %bitcast.18, bf16[256,128]{1,0:T(8,128)(2,1)} %bitcast.15, bf16[256,128]{1,0:T(8,128)(2,1)} %bitcast.16, ...), custom_call_target="tpu_custom_call" | custom-call | tf_op jit(solution)/shard_map/attend_whole/pallas_call | solution.py:650
  81.0 1.9 %write_results.1 = (bf16[256,512]{1,0:T(8,128)(2,1)}, bf16[256,512]{1,0:T(8,128)(2,1)}, bf16[256,128]{1,0:T(8,128)(2,1)}, bf16[256,128]{1,0:T(8,128)(2,1)}, f32[4,256]{1,0:T(4,128)}, /*index=5*/f32[2,128]{1,0:T(2,128)}) custom-call(bf16[256,512]{1,0:T(8,128)(2,1)} %get-tuple-element.18.refs_0_, bf16[256,512]{1,0:T(8,128)(2,1)} %get-tuple-element.19.refs_1_, ...), custom_call_target="tpu_custom_call" | custom-call | tf_op jit(solution)/shard_map/write_results/pallas_call | solution.py:705

commit v4 on v3

--- a/solution.py
+++ b/solution.py
@@ -25,6 +25,10 @@
 LN2 = math.log(2.0)
 FAR = (2, -1, 1, 0)
 BACK = 24
+FORWARD = (
+    (0, 0), (-1, 0), (0, -1), (1, 0), (0, 1), (2, 0), (0, 2), (-1, -1),
+    (-1, 1), (1, -1), (1, 1), (2, -1), (-1, 2), (2, 1), (1, 2), (2, 2),
+)
 ORDER = (
     (0, 0), (-1, 0), (0, -1), (1, 0), (0, 1), (-1, -1), (-1, 1), (1, -1),
     (1, 1), (2, 0), (0, 2), (2, -1), (-1, 2), (2, 1), (1, 2), (2, 2),
@@ -106,7 +110,7 @@
 
 
 def step_of(tree, da, db):
-    return ORDER.index((da, db) if tree == 0 else (db, da))
+    return FORWARD.index((da, db) if tree == 0 else (db, da))
 
 
 def fused_kernel(
@@ -134,7 +138,6 @@
     prob,
     score_low,
     out_sum,
-    key_gain_sum,
     offset,
     parts,
     twin,
@@ -300,15 +303,18 @@
             wait(tree, ("B2b", da), da, 2, "b")
             share(tree, da, 2)
 
+    def cross():
+        near(1)
+        far(0)
+
     gather_steps = {
-        0: axis_far,
-        1: functools.partial(near, -1),
-        2: functools.partial(near, 1),
-        3: functools.partial(far, 0),
-        4: functools.partial(near, 2),
-        5: functools.partial(far, -1),
-        6: functools.partial(far, 1),
-        7: functools.partial(far, 2),
+        2: axis_far,
+        4: functools.partial(near, -1),
+        5: cross,
+        7: functools.partial(near, 2),
+        9: functools.partial(far, -1),
+        11: functools.partial(far, 1),
+        13: functools.partial(far, 2),
     }
 
 
@@ -331,7 +337,6 @@
         query_turned[:, head * TOK : (head + 1) * TOK] = turn(normed.astype(F32)).astype(BF16)
         query_wide[head] = jnp.concatenate([normed, split_lanes(own_gate)], axis=1)
     out_sum[...] = jnp.zeros_like(out_sum)
-    key_gain_sum[...] = jnp.zeros_like(key_gain_sum)
     offset[...] = jnp.zeros_like(offset)
     lane_token = lax.broadcasted_iota(jnp.int32, (1, TOK), 1)
 
@@ -378,11 +383,11 @@
         carry = carry - jnp.where(shard < me, chunk, 0.0)
         base[shard] = carry
 
-    def chip_of(step):
-        return pick(step, [cells[entry] for entry in ORDER])
+    def chip_of(step, order):
+        return pick(step, [cells[entry] for entry in order])
 
     def forward_step(step, _):
-        cell = chip_of(step)
+        cell = chip_of(step, FORWARD)
 
         for at, action in gather_steps.items():
             pl.when(step == at)(action)
@@ -516,7 +521,6 @@
         value_part = jnp.dot(grad_turned[...], prob[me - block], preferred_element_type=F32)
         parts[block, HEAD_ROWS : HEAD_ROWS + DH, :] = key_part
         parts[block, HEAD_ROWS + DH :, :] = value_part.astype(BF16)
-        key_gain_sum[...] += jnp.dot(key_part, keys, preferred_element_type=F32)
         columns = jnp.concatenate(sums + [jnp.zeros((4, TOK), F32)], axis=0)
         high = columns.astype(BF16).astype(F32)
         parts[block, 0:HEAD_ROWS, :] = jnp.concatenate([-high, high - columns], axis=0).astype(BF16)
@@ -526,7 +530,7 @@
 
     def backward_step(turn, _):
         step = STEPS - 1 - turn
-        cell = chip_of(step)
+        cell = chip_of(step, ORDER)
 
         def one(which, _):
             block = cell * 2 + jnp.where(which == 1, core, 1 - core)
@@ -574,10 +578,7 @@
         turned.append(jnp.concatenate(halves, axis=1))
     row_sums = jnp.concatenate(turned, axis=0)
     query_gain_sum = query_gain_sum * (DH**-0.5)
-    row = lax.broadcasted_iota(jnp.int32, (DH, DH), 0)
-    col = lax.broadcasted_iota(jnp.int32, (DH, DH), 1)
-    diagonal = jnp.where(row == col, key_gain_sum[...], 0.0)
-    key_gain_row = jnp.sum(diagonal, axis=0, keepdims=True) / key_gain_ref[...]
+    key_gain_row = query_gain_sum * query_gain_ref[...] / key_gain_ref[...]
     small[0] = jnp.concatenate(
         [query_gain_sum, key_gain_row, jnp.zeros((6, DH), F32), offset[...]], axis=0
     )
@@ -670,7 +671,6 @@
             pltpu.VMEM((BACK + 1, rows, TOK), BF16),
             pltpu.VMEM((rows, TOK), BF16),
             pltpu.VMEM((HEADS, TOK, 2 * DH), F32),
-            pltpu.VMEM((DH, DH), F32),
             pltpu.VMEM((8, DH), F32),
             pltpu.VMEM((SHARDS, ROWS, 2 * DH), BF16),
             pltpu.VMEM((SHARDS // 2, ROWS, 2 * DH), BF16),

time: 83.4 us -> 78.2 us (0.938)
  Pallas kernels: 82.2 us -> 77.3 us
    pallas_call x1, Pallas kernels: 80.3 us -> 75.4 us  [fused(): pl.pallas_call(fused_kernel, out_shape=(wide, wide, narrow, narrow, jax.S...]
where the time goes in v4:
time: 78.2 us; the launch traced here: 77.9 us
  Pallas kernels  77.3 us (99%)
    pallas_call x1, Pallas kernels, fused(): pl.pallas_call(fused_kernel, out_shape=(wide, wide, narrow, narrow, jax.S...  75.4 us
    pallas_call x1, Pallas kernels, write(): pl.pallas_call(write_kernel, out_shape=tuple((jax.ShapeDtypeStruct(a.shap...  1.92 us

profile of v4, /device:TPU:0, one launch (start us, length us, event | category | flops | bytes accessed | tf_op | source)
XLA Modules:
  0.0 77.9 jit_solution(9719117549039517834)
XLA Ops:
  0.6 75.4 %attend_whole.1 = (bf16[256,512]{1,0:T(8,128)(2,1)}, bf16[256,512]{1,0:T(8,128)(2,1)}, bf16[256,128]{1,0:T(8,128)(2,1)}, bf16[256,128]{1,0:T(8,128)(2,1)}, f32[4,256]{1,0:T(4,128)}, /*index=5*/f32[2,128]{1,0:T(2,128)}) custom-call(s32[4]{0:T(128)} %bitcast.18, bf16[256,128]{1,0:T(8,128)(2,1)} %bitcast.15, bf16[256,128]{1,0:T(8,128)(2,1)} %bitcast.16, ...), custom_call_target="tpu_custom_call" | custom-call | tf_op jit(solution)/shard_map/attend_whole/pallas_call | solution.py:651
  76.0 1.9 %write_results.1 = (bf16[256,512]{1,0:T(8,128)(2,1)}, bf16[256,512]{1,0:T(8,128)(2,1)}, bf16[256,128]{1,0:T(8,128)(2,1)}, bf16[256,128]{1,0:T(8,128)(2,1)}, f32[4,256]{1,0:T(4,128)}, /*index=5*/f32[2,128]{1,0:T(2,128)}) custom-call(bf16[256,512]{1,0:T(8,128)(2,1)} %get-tuple-element.18.refs_0_, bf16[256,512]{1,0:T(8,128)(2,1)} %get-tuple-element.19.refs_1_, ...), custom_call_target="tpu_custom_call" | custom-call | tf_op jit(solution)/shard_map/write_results/pallas_call | solution.py:705

commit v5 on v4

--- a/solution.py
+++ b/solution.py
@@ -29,6 +29,7 @@
     (0, 0), (-1, 0), (0, -1), (1, 0), (0, 1), (2, 0), (0, 2), (-1, -1),
     (-1, 1), (1, -1), (1, 1), (2, -1), (-1, 2), (2, 1), (1, 2), (2, 2),
 )
+HELD = 5
 ORDER = (
     (0, 0), (-1, 0), (0, -1), (1, 0), (0, 1), (-1, -1), (-1, 1), (1, -1),
     (1, 1), (2, 0), (0, 2), (2, -1), (-1, 2), (2, 1), (1, 2), (2, 2),
@@ -139,6 +140,7 @@
     score_low,
     out_sum,
     offset,
+    row_sums,
     parts,
     twin,
     total,
@@ -499,7 +501,7 @@
         return [reduce_item(*item) for item in now]
 
 
-    def backward_block(block):
+    def score_block(block, slot):
         keys = shards[block, HEAD_ROWS:, 0:DH]
         values = shards[block, HEAD_ROWS:, DH:]
         key_wide = jnp.concatenate([keys, ones], axis=1)
@@ -515,12 +517,8 @@
             low = score_grad.astype(BF16)
             folded = jnp.sum(low.astype(F32).reshape(TOK // 8, 8, TOK), axis=0)
             sums.append(jnp.sum(folded, axis=0, keepdims=True))
-            score_low[span, :] = low
+            score_low[slot, span, :] = low
             out_sum[head] += jnp.dot(low, key_wide, preferred_element_type=F32)
-        key_part = (jnp.dot(query_turned[...], score_low[...], preferred_element_type=F32) * LN2).astype(BF16)
-        value_part = jnp.dot(grad_turned[...], prob[me - block], preferred_element_type=F32)
-        parts[block, HEAD_ROWS : HEAD_ROWS + DH, :] = key_part
-        parts[block, HEAD_ROWS + DH :, :] = value_part.astype(BF16)
         columns = jnp.concatenate(sums + [jnp.zeros((4, TOK), F32)], axis=0)
         high = columns.astype(BF16).astype(F32)
         parts[block, 0:HEAD_ROWS, :] = jnp.concatenate([-high, high - columns], axis=0).astype(BF16)
@@ -528,17 +526,46 @@
         whole = jnp.broadcast_to(jnp.sum(columns, axis=1, keepdims=True), (8, DH))
         offset[...] += jnp.where((lane >= block) & (lane < me), whole, 0.0)
 
-    def backward_step(turn, _):
+    def product_block(block, slot):
+        key_part = jnp.dot(query_turned[...], score_low[slot], preferred_element_type=F32) * LN2
+        value_part = jnp.dot(grad_turned[...], prob[me - block], preferred_element_type=F32)
+        parts[block, HEAD_ROWS : HEAD_ROWS + DH, :] = key_part.astype(BF16)
+        parts[block, HEAD_ROWS + DH :, :] = value_part.astype(BF16)
+
+    def block_of(cell, which):
+        block = cell * 2 + jnp.where(which == 1, core, 1 - core)
+        return block, (block <= me) & (block >= me - BACK)
+
+    def small_copies(axis):
+        return [
+            remote(small.at[axis], small_landed.at[7 * axis + i], small_send, small_recv, 7 * axis + i, device)
+            for i, device in enumerate(partners[axis])
+        ]
+
+    def small_add(axis):
+        whole = small[axis]
+        shared = lax.broadcasted_iota(jnp.int32, (16, DH), 0) < 8
+        for i, made in enumerate(small_copies(axis)):
+            made.wait_recv()
+            term = small_landed[7 * axis + i]
+            if axis == 1 and field_steps[i][1]:
+                term = jnp.where(shared, term, 0.0)
+            whole = whole + term
+        small[axis + 1] = whole
+
+    def backward_step(held, turn, _):
         step = STEPS - 1 - turn
         cell = chip_of(step, ORDER)
 
         def one(which, _):
-            block = cell * 2 + jnp.where(which == 1, core, 1 - core)
-            used = (block <= me) & (block >= me - BACK)
+            block, used = block_of(cell, which)
+            slot = step * 2 + which if held else 0
 
             @pl.when(used)
             def _():
-                backward_block(block)
+                if not held:
+                    score_block(block, slot)
+                product_block(block, slot)
 
             @pl.when(jnp.logical_not(used))
             def _():
@@ -551,15 +578,36 @@
             return 0
 
         lax.fori_loop(0, 2, one, 0)
-        for at in range(1, STEPS):
+        first = STEPS - HELD
+        for at in range(first + 1, STEPS) if held else range(1, first):
 
             @pl.when(turn == at)
             def _():
                 reduce_turn(at)
+                if at == STEPS - 2:
+                    small_add(0)
+                    for made in small_copies(1):
+                        made.start()
 
         return 0
 
-    lax.fori_loop(0, STEPS, backward_step, 0)
+    def held_step(step, _):
+        cell = chip_of(step, ORDER)
+
+        def one(which, _):
+            block, used = block_of(cell, which)
+
+            @pl.when(used)
+            def _():
+                score_block(block, step * 2 + which)
+
+            return 0
+
+        return lax.fori_loop(0, 2, one, 0)
+
+    lax.fori_loop(0, STEPS - HELD, functools.partial(backward_step, False), 0)
+    lax.fori_loop(0, HELD, held_step, 0)
+    reduce_turn(STEPS - HELD)
 
 
     query_gain_sum = jnp.zeros((1, DH), F32)
@@ -576,36 +624,17 @@
         query_grad_ref[:, span] = (scale * (inner - hat * mean)).astype(BF16)
         halves = [jnp.transpose(out_sum[head, half * DH : (half + 1) * DH, DH:])[0:1] for half in (0, 1)]
         turned.append(jnp.concatenate(halves, axis=1))
-    row_sums = jnp.concatenate(turned, axis=0)
+    row_sums[...] = jnp.concatenate(turned, axis=0)
     query_gain_sum = query_gain_sum * (DH**-0.5)
     key_gain_row = query_gain_sum * query_gain_ref[...] / key_gain_ref[...]
     small[0] = jnp.concatenate(
         [query_gain_sum, key_gain_row, jnp.zeros((6, DH), F32), offset[...]], axis=0
     )
 
-    def small_copies(axis):
-        return [
-            remote(small.at[axis], small_landed.at[7 * axis + i], small_send, small_recv, 7 * axis + i, device)
-            for i, device in enumerate(partners[axis])
-        ]
-
-    def small_add(axis):
-        whole = small[axis]
-        shared = lax.broadcasted_iota(jnp.int32, (16, DH), 0) < 8
-        for i, made in enumerate(small_copies(axis)):
-            made.wait_recv()
-            term = small_landed[7 * axis + i]
-            if axis == 1 and field_steps[i][1]:
-                term = jnp.where(shared, term, 0.0)
-            whole = whole + term
-        small[axis + 1] = whole
-
     for made in small_copies(0):
         made.start()
+    lax.fori_loop(STEPS - HELD, STEPS, functools.partial(backward_step, True), 0)
     finals = reduce_turn(STEPS)
-    small_add(0)
-    for made in small_copies(1):
-        made.start()
 
     value_grad_ref[...] = turn(finals[1]).astype(BF16)
     cotangent = turn(finals[0][HEAD_ROWS:])
@@ -616,7 +645,7 @@
     mean = jnp.mean(inner * hat, axis=1, keepdims=True)
     key_grad_ref[...] = (scale * (inner - hat * mean)).astype(BF16)
 
-    gates = finals[0][0:4] + finals[0][8:12] + row_sums
+    gates = finals[0][0:4] + finals[0][8:12] + row_sums[...]
     row = lax.broadcasted_iota(jnp.int32, (TOK, TOK), 0)
     col = lax.broadcasted_iota(jnp.int32, (TOK, TOK), 1)
     lower = (row >= col).astype(F32)
@@ -669,9 +698,10 @@
             pltpu.VMEM((HEADS, TOK, 2 * DH), BF16),
             pltpu.VMEM((DH, rows), BF16),
             pltpu.VMEM((BACK + 1, rows, TOK), BF16),
-            pltpu.VMEM((rows, TOK), BF16),
+            pltpu.VMEM((2 * HELD, rows, TOK), BF16),
             pltpu.VMEM((HEADS, TOK, 2 * DH), F32),
             pltpu.VMEM((8, DH), F32),
+            pltpu.VMEM((HEADS, TOK), F32),
             pltpu.VMEM((SHARDS, ROWS, 2 * DH), BF16),
             pltpu.VMEM((SHARDS // 2, ROWS, 2 * DH), BF16),
             pltpu.VMEM((SHARDS // 2, ROWS, 2 * DH), BF16),

time: 78.2 us -> 75.2 us (0.962)
  Pallas kernels: 77.3 us -> 73.9 us
    pallas_call x1, Pallas kernels: 75.4 us -> 72 us  [fused(): pl.pallas_call(fused_kernel, out_shape=(wide, wide, narrow, narrow, jax.S...]
where the time goes in v5:
time: 75.2 us; the launch traced here: 74.6 us
  Pallas kernels  73.9 us (98%)
    pallas_call x1, Pallas kernels, fused(): pl.pallas_call(fused_kernel, out_shape=(wide, wide, narrow, narrow, jax.S...  72 us
    pallas_call x1, Pallas kernels, write(): pl.pallas_call(write_kernel, out_shape=tuple((jax.ShapeDtypeStruct(a.shap...  1.92 us

profile of v5, /device:TPU:0, one launch (start us, length us, event | category | flops | bytes accessed | tf_op | source)
XLA Modules:
  0.0 74.6 jit_solution(15600142912894398449)
XLA Ops:
  0.6 72.0 %attend_whole.1 = (bf16[256,512]{1,0:T(8,128)(2,1)}, bf16[256,512]{1,0:T(8,128)(2,1)}, bf16[256,128]{1,0:T(8,128)(2,1)}, bf16[256,128]{1,0:T(8,128)(2,1)}, f32[4,256]{1,0:T(4,128)}, /*index=5*/f32[2,128]{1,0:T(2,128)}) custom-call(s32[4]{0:T(128)} %bitcast.18, bf16[256,128]{1,0:T(8,128)(2,1)} %bitcast.15, bf16[256,128]{1,0:T(8,128)(2,1)} %bitcast.16, ...), custom_call_target="tpu_custom_call" | custom-call | tf_op jit(solution)/shard_map/attend_whole/pallas_call | solution.py:680
  72.6 1.9 %write_results.1 = (bf16[256,512]{1,0:T(8,128)(2,1)}, bf16[256,512]{1,0:T(8,128)(2,1)}, bf16[256,128]{1,0:T(8,128)(2,1)}, bf16[256,128]{1,0:T(8,128)(2,1)}, f32[4,256]{1,0:T(4,128)}, /*index=5*/f32[2,128]{1,0:T(2,128)}) custom-call(bf16[256,512]{1,0:T(8,128)(2,1)} %get-tuple-element.18.refs_0_, bf16[256,512]{1,0:T(8,128)(2,1)} %get-tuple-element.19.refs_1_, ...), custom_call_target="tpu_custom_call" | custom-call | tf_op jit(solution)/shard_map/write_results/pallas_call | solution.py:735

commit v6 on v5

--- a/solution.py
+++ b/solution.py
@@ -49,13 +49,6 @@
 def rows_of(tree, part):
     first, count = piece(tree, part)
     return pl.ds(first, count)
-
-
-def greet(devices):
-    barrier = pltpu.get_barrier_semaphore()
-    for device in devices:
-        pl.semaphore_signal(barrier, inc=1, device_id=device, device_id_type=MESH)
-    pl.semaphore_wait(barrier, len(devices))
 
 
 def ring_events():
@@ -181,7 +174,10 @@
         [(zs[dz] * 8 + y * 2 + (other if dc else core), rep) for dz, dc in line_steps],
         [(z * 8 + ys[dy] * 2 + core, reps[dx]) for dy, dx in field_steps],
     ]
-    greet([device for group in partners for device in group])
+    met = [device for group in partners for device in group]
+    barrier = pltpu.get_barrier_semaphore()
+    for device in met:
+        pl.semaphore_signal(barrier, inc=1, device_id=device, device_id_type=MESH)
 
     def remote(source, target, sends, receives, number, device):
         return pltpu.make_async_remote_copy(
@@ -209,6 +205,7 @@
     mid = (local - high).astype(BF16).astype(F32)
     packed = [high, mid, local - high - mid, jnp.zeros((4, TOK), F32)]
     shards[me, 0:HEAD_ROWS, :] = jnp.concatenate(packed, axis=0).astype(BF16)
+    pl.semaphore_wait(barrier, len(met))
 
     ids = {}
     for tree in (0, 1):
@@ -234,10 +231,6 @@
     def wait(tree, name, da, db, part):
         place = shards.at[shard_at(tree, da, db), rows_of(tree, part)]
         remote(place, place, out_send, out_recv, ids[tree, name], sibling).wait_recv()
-
-    for tree in (0, 1):
-        send((tree, "A-"), tree, 0, 0, "ab", (1, 0))
-        send((tree, "A+"), tree, 0, 0, "ab", (-1, 0))
 
     line = z * 2 + core
     chunk_sum[y, line] = jnp.concatenate(
@@ -266,6 +259,10 @@
 
     for made in sum_copies(0):
         made.start()
+    for tree in (0, 1):
+        send((tree, "A-"), tree, 0, 0, "ab", (1, 0))
+        send((tree, "A+"), tree, 0, 0, "ab", (-1, 0))
+
     for tree in (0, 1):
         send((tree, ("B-", 0)), tree, 0, 0, "ab", (0, 1))
         send((tree, ("B+", 0)), tree, 0, 0, "ab", (0, -1))

time: 75.2 us -> 73.8 us (0.981)
  Pallas kernels: 73.9 us -> 72.3 us
    pallas_call x1, Pallas kernels: 72 us -> 70.3 us  [fused(): pl.pallas_call(fused_kernel, out_shape=(wide, wide, narrow, narrow, jax.S...]
where the time goes in v6:
time: 73.8 us; the launch traced here: 72.9 us
  Pallas kernels  72.3 us (98%)
    pallas_call x1, Pallas kernels, fused(): pl.pallas_call(fused_kernel, out_shape=(wide, wide, narrow, narrow, jax.S...  70.3 us
    pallas_call x1, Pallas kernels, write(): pl.pallas_call(write_kernel, out_shape=tuple((jax.ShapeDtypeStruct(a.shap...  1.92 us

profile of v6, /device:TPU:0, one launch (start us, length us, event | category | flops | bytes accessed | tf_op | source)
XLA Modules:
  0.0 72.9 jit_solution(6425563890772607388)
XLA Ops:
  0.6 70.3 %attend_whole.1 = (bf16[256,512]{1,0:T(8,128)(2,1)}, bf16[256,512]{1,0:T(8,128)(2,1)}, bf16[256,128]{1,0:T(8,128)(2,1)}, bf16[256,128]{1,0:T(8,128)(2,1)}, f32[4,256]{1,0:T(4,128)}, /*index=5*/f32[2,128]{1,0:T(2,128)}) custom-call(s32[4]{0:T(128)} %bitcast.18, bf16[256,128]{1,0:T(8,128)(2,1)} %bitcast.15, bf16[256,128]{1,0:T(8,128)(2,1)} %bitcast.16, ...), custom_call_target="tpu_custom_call" | custom-call | tf_op jit(solution)/shard_map/attend_whole/pallas_call | solution.py:677
  71.0 1.9 %write_results.1 = (bf16[256,512]{1,0:T(8,128)(2,1)}, bf16[256,512]{1,0:T(8,128)(2,1)}, bf16[256,128]{1,0:T(8,128)(2,1)}, bf16[256,128]{1,0:T(8,128)(2,1)}, f32[4,256]{1,0:T(4,128)}, /*index=5*/f32[2,128]{1,0:T(2,128)}) custom-call(bf16[256,512]{1,0:T(8,128)(2,1)} %get-tuple-element.18.refs_0_, bf16[256,512]{1,0:T(8,128)(2,1)} %get-tuple-element.19.refs_1_, ...), custom_call_target="tpu_custom_call" | custom-call | tf_op jit(solution)/shard_map/write_results/pallas_call | solution.py:732
